TPU v7x, 128 devices: a whole 4x4x4 slice. The times are simulated.
128 devices in a mesh: seq: 16 (over y, x), mp: 4 (over z), section: 2 (over core).
Axes of the slice: x: 4, y: 4, z: 4, core: 2. Of those that a mesh axis runs over, the one named last changes fastest.
Arguments:
- out_grad: bfloat16 [8192, 4608], P('seq', ('mp', 'section')), may hold values from -6 to 6
- out_weight: bfloat16 [4096, 4608], P(None, ('mp', 'section')), may hold values from -0.09375 to 0.09375
- query_states: bfloat16 [8192, 4096], P('seq', ('mp', 'section')), may hold values from -6 to 6
- key_states: bfloat16 [8192, 2048], P('seq', ('mp', 'section')), may hold values from -6 to 6
- value_states: bfloat16 [8192, 2048], P('seq', ('mp', 'section')), may hold values from -6 to 6
- slot_seq: int32 [128], replicated, may hold values from 0 to 16, as said below
- slot_pos: int32 [128], replicated, may hold values from 0 to 15, as said below
- fork_depth: int32 [16], replicated, may hold values from 1 to 16, as said below
Outputs:
- query_grad: bfloat16 [8192, 4096], P('seq', ('mp', 'section'))
- key_grad: bfloat16 [8192, 2048], P('seq', ('mp', 'section'))
- value_grad: bfloat16 [8192, 2048], P('seq', ('mp', 'section'))
Inputs may be any that keep to these rules, and one draw needn't show every extreme that they name: `slot_seq`: blocks are listed device by device, 8 to a device along seq. Every device holds all blocks of exactly one response and fills its other slots with prompt blocks, at most 2 of them and exactly 2 on some device; as many devices hold 2 prompt blocks as hold none. Each of the 16 responses and each of the 16 prompt blocks appears once. Slots are in no particular order. `slot_pos`: prompt blocks carry indices 0 to 15; a response's blocks are numbered from 0 without gaps. `fork_depth`: some response sees the whole prompt and some other response only its first block.
All inputs are finite; a program needn't handle non-finite values.
Results may differ from a plain program's by a relative error of at most 0.017.
Values may be sent and summed in bfloat16 or wider, within the bound.
No kernel may reach another device: no remote copies, remote signals or barrier semaphores. Data moves between devices by JAX's collectives and lax.ppermute only.
A program may use at most 128 MiB of HBM per device.

v0:
```python
import jax
import jax.numpy as jnp
from jax import lax
from jax.sharding import PartitionSpec as P

HD = 128
BLK = 64
BLK_DEV = 8
PCAP = 2


SCALE = 144.0 ** (-0.5)
SOFTCAP = 50.0


def allowed(qseq, qpos, qdepth, kseq, kpos):
    qs = qseq[:, None]
    qp = qpos[:, None]
    ks = kseq[None, :]
    kp = kpos[None, :]
    prompt_key = jnp.where(qs == 0, kp <= qp, kp < qdepth[:, None])
    own_key = (ks == qs) & (kp <= qp)
    return jnp.where(ks == 0, prompt_key, own_key)


def scores(queries, head_grad, key_value, mask):
    width = key_value.shape[0]
    heads = queries.shape[1]
    key_part = key_value[:, : heads * HD].reshape(width, heads, HD)
    value_part = key_value[:, heads * HD :].reshape(width, heads, HD)
    raw = (
        jnp.einsum("nagd,mad->agnm", queries, key_part, preferred_element_type=jnp.float32) * SCALE
    )
    tanh_val = jnp.tanh(raw / SOFTCAP)
    expo = jnp.where(mask[None, None], jnp.exp(SOFTCAP * tanh_val), 0.0)
    dprob = jnp.einsum("agdn,mad->agnm", head_grad, value_part, preferred_element_type=jnp.float32)
    return (tanh_val, expo, dprob, key_part)


def stats_add(carry, queries, head_grad, key_value, mask):
    total, weighted = carry
    tanh_val, expo, dprob, key_part = scores(queries, head_grad, key_value, mask)
    return (total + jnp.sum(expo, axis=-1), weighted + jnp.sum(expo * dprob, axis=-1))


def grads(queries, head_grad, key_value, mask, total, delta):
    tanh_val, expo, dprob, key_part = scores(queries, head_grad, key_value, mask)
    width = key_value.shape[0]
    prob = expo / total[..., None]
    dscore = prob * (dprob - delta[..., None]) * (1.0 - tanh_val * tanh_val) * SCALE
    prob16 = prob.astype(jnp.bfloat16)
    dscore16 = dscore.astype(jnp.bfloat16)
    dquery = jnp.einsum("agnm,mad->nagd", dscore16, key_part, preferred_element_type=jnp.float32)
    dkey = jnp.einsum("agnm,nagd->mad", dscore16, queries, preferred_element_type=jnp.float32)
    dvalue = jnp.einsum("agnm,agdn->mad", prob16, head_grad, preferred_element_type=jnp.float32)
    return (dquery, jnp.concatenate([dkey.reshape(width, -1), dvalue.reshape(width, -1)], axis=1))


def shards(
    out_grad, out_weight, query_states, key_states, value_states, slot_seq, slot_pos, fork_depth
):
    rows = query_states.shape[0]
    kv_heads = key_states.shape[1] // HD
    group = query_states.shape[1] // (kv_heads * HD)
    devices = lax.axis_size("seq")
    here = lax.axis_index("seq")
    summed = lax.psum_scatter(
        jnp.einsum("cd,td->ct", out_weight, out_grad, preferred_element_type=jnp.float32),
        ("mp", "section"),
        scatter_dimension=0,
        tiled=True,
    )
    head_grad = summed.astype(jnp.bfloat16).reshape(kv_heads, group, HD, rows)
    queries = query_states.reshape(rows, kv_heads, group, HD)
    offset = jnp.arange(BLK, dtype=jnp.int32)
    seq_all = slot_seq.reshape(devices, BLK_DEV)
    pos_all = slot_pos.reshape(devices, BLK_DEV)
    is_prompt = (seq_all == 0).astype(jnp.int32)
    rank = jnp.cumsum(is_prompt, axis=1) - 1
    capacity = jnp.arange(PCAP, dtype=jnp.int32)
    pick = (is_prompt[:, None, :] == 1) & (rank[:, None, :] == capacity[None, :, None])
    slot_valid = jnp.any(pick, axis=2).reshape(-1)
    slot_ppos = jnp.sum(jnp.where(pick, pos_all[:, None, :], 0), axis=2).reshape(-1)
    own_pick = lax.dynamic_index_in_dim(pick, here, 0, keepdims=False)
    local_seq = lax.dynamic_slice_in_dim(slot_seq, here * BLK_DEV, BLK_DEV, 0)
    local_pos = lax.dynamic_slice_in_dim(slot_pos, here * BLK_DEV, BLK_DEV, 0)
    qseq = jnp.repeat(local_seq, BLK)
    qpos = (local_pos[:, None] * BLK + offset[None, :]).reshape(-1)
    branch = jnp.arange(fork_depth.shape[0], dtype=jnp.int32) + 1
    table = (qseq[:, None] == branch[None, :]).astype(jnp.int32)
    qdepth = jnp.sum(table * fork_depth[None, :], axis=1) * BLK
    local_kseq = jnp.where(qseq == 0, -1, qseq)
    local_mask = allowed(qseq, qpos, qdepth, local_kseq, qpos)
    key_value = jnp.concatenate([key_states, value_states], axis=1)
    feat = key_value.shape[1]
    blocks = key_value.reshape(BLK_DEV, BLK, feat)
    prompt_buf = jnp.einsum(
        "cs,sbw->cbw", own_pick.astype(jnp.bfloat16), blocks, preferred_element_type=jnp.float32
    ).astype(jnp.bfloat16)
    prompt_kseq = jnp.repeat(jnp.where(slot_valid, 0, -1), BLK)
    prompt_kpos = (slot_ppos[:, None] * BLK + offset[None, :]).reshape(-1)
    slots_local = prompt_buf.shape[0]
    slots_all = devices * slots_local
    zero_stats = jnp.zeros((kv_heads, group, rows), jnp.float32)
    stats = stats_add((zero_stats, zero_stats), queries, head_grad, key_value, local_mask)
    gathered = lax.all_gather(prompt_buf, "seq", axis=0, tiled=True).reshape(slots_all * BLK, feat)
    key_total = slots_all * BLK
    key_block = 512
    nkb = key_total // key_block
    tiles = gathered.reshape(nkb, key_block, feat)
    tile_seq = prompt_kseq.reshape(nkb, key_block)
    tile_pos = prompt_kpos.reshape(nkb, key_block)

    def pass_one(carry, block):
        tile, bseq, bpos = block
        mask = allowed(qseq, qpos, qdepth, bseq, bpos)
        return (stats_add(carry, queries, head_grad, tile, mask), None)

    stats, unused = lax.scan(pass_one, stats, (tiles, tile_seq, tile_pos))
    total, weighted = stats
    delta = weighted / total
    dquery, local_kv_grad = grads(queries, head_grad, key_value, local_mask, total, delta)

    def pass_two(acc, block):
        tile, bseq, bpos = block
        mask = allowed(qseq, qpos, qdepth, bseq, bpos)
        dquery_b, dkv_b = grads(queries, head_grad, tile, mask, total, delta)
        return (acc + dquery_b, dkv_b)

    dquery, prompt_terms = lax.scan(pass_two, dquery, (tiles, tile_seq, tile_pos))
    prompt_terms = prompt_terms.reshape(slots_all, BLK, feat)
    returned = lax.psum_scatter(
        prompt_terms.astype(jnp.bfloat16), "seq", scatter_dimension=0, tiled=True
    ).astype(jnp.float32)
    back = jnp.einsum(
        "cs,cbw->sbw", own_pick.astype(jnp.float32), returned, precision=lax.Precision.HIGHEST
    ).reshape(rows, feat)
    kv_grad = local_kv_grad + back
    half = kv_heads * HD
    query_grad = dquery.reshape(rows, -1).astype(jnp.bfloat16)
    key_grad = kv_grad[:, :half].astype(jnp.bfloat16)
    value_grad = kv_grad[:, half:].astype(jnp.bfloat16)
    return (query_grad, key_grad, value_grad)


def solution(mesh):
    return jax.shard_map(
        shards,
        mesh=mesh,
        in_specs=(
            P("seq", ("mp", "section")),
            P(None, ("mp", "section")),
            P("seq", ("mp", "section")),
            P("seq", ("mp", "section")),
            P("seq", ("mp", "section")),
            P(),
            P(),
            P(),
        ),
        out_specs=(
            P("seq", ("mp", "section")),
            P("seq", ("mp", "section")),
            P("seq", ("mp", "section")),
        ),
        check_vma=False,
    )
```

profile of v0, /device:TPU:0, one launch (start us, length us, event | category | flops | bytes accessed | tf_op | source)
XLA Modules:
  0.0 235.2 jit_solution(15036038356087920281)
XLA Ops:
  12.4 8.2 %fusion.47 = f32[4096,512]{1,0:T(8,128)} fusion(bf16[4096,576]{0,1:T(8,128)(2,1)} %param.13, bf16[512,576]{0,1:T(8,128)(2,1)S(1)} %copy-done), kind=kOutput, calls=%fused_computation.94 | convolution fusion | flops 2415919104 | bytes 13697024 | tf_op jit(solution)/shard_map/cd,td->ct/dot_general | solution.py:68
  26.2 2.7 %fusion.33 = f32[2,512,512,2]{2,1,3,0:T(8,128)} fusion(bf16[512,2,2,128]{0,3,2,1:T(8,128)(2,1)S(1)} %bitcast.216, bf16[512,2,128,1]{2,1,0,3:T(2,128)(2,1)S(1)} %bitcast.225), kind=kOutput, calls=%fused_computation.64 | convolution fusion | flops 268435456 | bytes 4980736 | tf_op jit(solution)/shard_map/nagd,mad->agnm/dot_general | solution.py:32
  28.9 31.0 %all-gather.2.cloned.1.call-done = bf16[32,64,512]{2,1,0:T(8,128)(2,1)} async-done(((bf16[2,64,512]{2,1,0:T(8,128)(2,1)}), bf16[32,64,512]{2,1,0:T(8,128)(2,1)}) %all-gather.2.cloned.1.call-update) | async-done | bytes 2097168 | tf_op jit(solution)/shard_map/all_gather | solution.py:106
  59.9 2.8 %copy.99 = bf16[4,512,512]{1,2,0:T(8,128)(2,1)S(1)} copy(bf16[4,512,512]{2,1,0:T(8,128)(2,1)} %bitcast.230) | data formatting | bytes 4194304
  62.8 13.0 %reduce-scatter.3.cloned.1.call-done = f32[512,512]{1,0:T(8,128)} async-done(((f32[4096,512]{1,0:T(8,128)}), f32[512,512]{1,0:T(8,128)}) %reduce-scatter.3.cloned.1.call-update) | async-done | bytes 1048592 | tf_op jit(solution)/shard_map/reduce_scatter | solution.py:67
  75.7 1.3 convert_element_type.56
  77.0 6.0 %multiply_reduce_fusion = (f32[2,2,512]{2,1,0:T(2,128)S(1)}, f32[2,2,512]{2,1,0:T(2,128)S(1)}, f32[2,2,512,512]{2,3,1,0:T(8,128)}) fusion(f32[2,512,512,2]{2,1,3,0:T(8,128)} %fusion.33, pred[512,512]{0,1:T(8,128)(4,1)} %fusion.28, bf16[2,2,128,512]{3,2,1,0:T(8,128)(2,1)S(1)} %bitcast.232, bf16[512,2,128,1]{2,1,0,3:T(2,128)(2,1)} %bitcast.235), kind=kOutput, calls=%fused_computation.46 | convolution fusion | flops 274722816 | bytes 9453568 | tf_op jit(solution)/shard_map/agdn,mad->agnm/dot_general | solution.py:36
  83.0 20.8 %while.30 = (s32[]{:T(128)}, f32[2,2,512]{2,1,0:T(2,128)S(1)}, f32[2,2,512]{2,1,0:T(2,128)S(1)}, s32[4,512]{1,0:T(4,128)S(1)}, s32[4,512]{1,0:T(4,128)S(1)}, /*i...) while((s32[]{:T(128)}, f32[2,2,512]{2,1,0:T(2,128)S(1)}, ...), condition=%wide.region_10.11_spmd.clone, body=%wide.region_7.10_spmd.clone.sunk | while | flops 547882496 | bytes 15042789 | solution.py:119
  84.0 2.6 %fusion.101 = (f32[2,2,512]{2,1,0:T(2,128)S(1)}, f32[2,512,512,2]{2,1,3,0:T(8,128)S(1)}) fusion(pred[512,512]{0,1:T(8,128)(4,1)S(1)} %fusion.99, bf16[512,2,128,1]{0,2,3,1:T(8,128)(2,1)S(1)} %bitcast.224, bf16[512,2,2,128]{3,0,2,1:T(8,128)(2,1)} %get-tuple-element.727), kind=kOutput, calls=%fused_computation.7.clone.1 | convolution fusion | flops 272627712 | bytes 5251072 | tf_op jit(solution)/shard_map/while/body/eval_jaxpr/nagd,mad->agnm/dot_general | solution.py:32
  86.6 1.6 fusion.102
  89.2 2.6 %fusion.101 = (f32[2,2,512]{2,1,0:T(2,128)S(1)}, f32[2,512,512,2]{2,1,3,0:T(8,128)S(1)}) fusion(pred[512,512]{0,1:T(8,128)(4,1)S(1)} %fusion.99, bf16[512,2,128,1]{0,2,3,1:T(8,128)(2,1)S(1)} %bitcast.224, bf16[512,2,2,128]{3,0,2,1:T(8,128)(2,1)} %get-tuple-element.727), kind=kOutput, calls=%fused_computation.7.clone.1 | convolution fusion | flops 272627712 | bytes 5251072 | tf_op jit(solution)/shard_map/while/body/eval_jaxpr/nagd,mad->agnm/dot_general | solution.py:32
  91.8 1.6 fusion.102
  94.4 2.6 %fusion.101 = (f32[2,2,512]{2,1,0:T(2,128)S(1)}, f32[2,512,512,2]{2,1,3,0:T(8,128)S(1)}) fusion(pred[512,512]{0,1:T(8,128)(4,1)S(1)} %fusion.99, bf16[512,2,128,1]{0,2,3,1:T(8,128)(2,1)S(1)} %bitcast.224, bf16[512,2,2,128]{3,0,2,1:T(8,128)(2,1)} %get-tuple-element.727), kind=kOutput, calls=%fused_computation.7.clone.1 | convolution fusion | flops 272627712 | bytes 5251072 | tf_op jit(solution)/shard_map/while/body/eval_jaxpr/nagd,mad->agnm/dot_general | solution.py:32
  97.0 1.6 fusion.102
  99.6 2.6 %fusion.101 = (f32[2,2,512]{2,1,0:T(2,128)S(1)}, f32[2,512,512,2]{2,1,3,0:T(8,128)S(1)}) fusion(pred[512,512]{0,1:T(8,128)(4,1)S(1)} %fusion.99, bf16[512,2,128,1]{0,2,3,1:T(8,128)(2,1)S(1)} %bitcast.224, bf16[512,2,2,128]{3,0,2,1:T(8,128)(2,1)} %get-tuple-element.727), kind=kOutput, calls=%fused_computation.7.clone.1 | convolution fusion | flops 272627712 | bytes 5251072 | tf_op jit(solution)/shard_map/while/body/eval_jaxpr/nagd,mad->agnm/dot_general | solution.py:32
  102.2 1.6 fusion.102
  103.9 5.2 %fusion.23 = bf16[2,2,512,512]{2,3,1,0:T(8,128)(2,1)S(1)} fusion(f32[2,2,512,512]{2,3,1,0:T(8,128)} %get-tuple-element.527, f32[2,512,512,2]{2,1,3,0:T(8,128)} %fusion.33, f32[2,2,512]{2,1,0:T(2,128)S(1)} %div.45, f32[2,2,512]{2,1,0:T(2,128)S(1)} %get-tuple-element.740, pred[512,512]{0,1:T(8,128)(4,1)} %fusion.28), kind=kLoop, calls=%fused_computation.44 | loop fusion | flops 11534336 | bytes 10764288 | tf_op jit(solution)/shard_map/convert_element_type | solution.py:52
  109.1 1.3 copy-done.2
  110.5 1.9 convolution_bitcast_fusion.1
  112.4 1.6 copy.103
  114.0 36.9 %while.31 = (s32[]{:T(128)}, f32[512,2,2,128]{0,3,2,1:T(8,128)S(1)}, bf16[4,512,512]{2,1,0:T(8,128)(2,1)}, bf16[4,512,512]{1,2,0:T(8,128)(2,1)}, s32[4,512]{1,0:...) while((s32[]{:T(128)}, ...), condition=%wide.region_12.13_spmd.clone, body=%wide.region_11.12_spmd.clone.sunk | while | flops 1361839616 | bytes 32565496 | solution.py:130
  116.9 1.5 fusion.118
  118.5 2.4 %fusion.116 = bf16[2,2,512,512]{2,3,1,0:T(8,128)(2,1)S(1)} fusion(f32[2,512,512,2]{2,1,3,0:T(8,128)S(1)} %fusion.114, bf16[512,2,128,1]{0,2,3,1:T(8,128)(2,1)S(1)} %bitcast.223, bf16[2,2,128,512]{3,2,1,0:T(8,128)(2,1)S(1)} %copy-done.8, f32[2,2,512]{2,1,0:T(2,128)S(1)} %get-tuple-element.770, f32[2,2,512]{2,1,0:T(2,128)S(1)} %get-tuple-element.768, ...), kind=kOutput, calls=%fused_computation.19.clone.1 | convolution fusion | flops 279969792 | bytes 7356416 | tf_op jit(solution)/shard_map/while/body/eval_jaxpr/agdn,mad->agnm/dot_general | solution.py:36
  126.1 1.5 fusion.118
  127.6 2.4 %fusion.116 = bf16[2,2,512,512]{2,3,1,0:T(8,128)(2,1)S(1)} fusion(f32[2,512,512,2]{2,1,3,0:T(8,128)S(1)} %fusion.114, bf16[512,2,128,1]{0,2,3,1:T(8,128)(2,1)S(1)} %bitcast.223, bf16[2,2,128,512]{3,2,1,0:T(8,128)(2,1)S(1)} %copy-done.8, f32[2,2,512]{2,1,0:T(2,128)S(1)} %get-tuple-element.770, f32[2,2,512]{2,1,0:T(2,128)S(1)} %get-tuple-element.768, ...), kind=kOutput, calls=%fused_computation.19.clone.1 | convolution fusion | flops 279969792 | bytes 7356416 | tf_op jit(solution)/shard_map/while/body/eval_jaxpr/agdn,mad->agnm/dot_general | solution.py:36
  135.3 1.5 fusion.118
  136.8 2.4 %fusion.116 = bf16[2,2,512,512]{2,3,1,0:T(8,128)(2,1)S(1)} fusion(f32[2,512,512,2]{2,1,3,0:T(8,128)S(1)} %fusion.114, bf16[512,2,128,1]{0,2,3,1:T(8,128)(2,1)S(1)} %bitcast.223, bf16[2,2,128,512]{3,2,1,0:T(8,128)(2,1)S(1)} %copy-done.8, f32[2,2,512]{2,1,0:T(2,128)S(1)} %get-tuple-element.770, f32[2,2,512]{2,1,0:T(2,128)S(1)} %get-tuple-element.768, ...), kind=kOutput, calls=%fused_computation.19.clone.1 | convolution fusion | flops 279969792 | bytes 7356416 | tf_op jit(solution)/shard_map/while/body/eval_jaxpr/agdn,mad->agnm/dot_general | solution.py:36
  144.5 1.5 fusion.118
  146.0 2.4 %fusion.116 = bf16[2,2,512,512]{2,3,1,0:T(8,128)(2,1)S(1)} fusion(f32[2,512,512,2]{2,1,3,0:T(8,128)S(1)} %fusion.114, bf16[512,2,128,1]{0,2,3,1:T(8,128)(2,1)S(1)} %bitcast.223, bf16[2,2,128,512]{3,2,1,0:T(8,128)(2,1)S(1)} %copy-done.8, f32[2,2,512]{2,1,0:T(2,128)S(1)} %get-tuple-element.770, f32[2,2,512]{2,1,0:T(2,128)S(1)} %get-tuple-element.768, ...), kind=kOutput, calls=%fused_computation.19.clone.1 | convolution fusion | flops 279969792 | bytes 7356416 | tf_op jit(solution)/shard_map/while/body/eval_jaxpr/agdn,mad->agnm/dot_general | solution.py:36
  151.0 3.8 %fusion.24 = f32[2,128,512,1]{2,1,3,0:T(8,128)S(1)} fusion(bf16[2,2,128,512]{3,2,1,0:T(8,128)(2,1)} %get-tuple-element.786, f32[2,2,512]{2,1,0:T(2,128)S(1)} %get-tuple-element.789, f32[2,512,512,2]{2,1,3,0:T(8,128)} %fusion.33, pred[512,512]{0,1:T(8,128)(4,1)S(1)} %copy-done.5), kind=kOutput, calls=%fused_computation.48 | convolution fusion | flops 273678336 | bytes 5513216 | tf_op jit(solution)/shard_map/agnm,agdn->mad/dot_general | solution.py:55
  155.0 2.4 %fusion.48 = f32[2,512,128,1]{1,2,3,0:T(8,128)S(1)} fusion(bf16[2,2,512,512]{2,3,1,0:T(8,128)(2,1)} %copy-done.2, bf16[512,2,2,128]{0,3,2,1:T(8,128)(2,1)S(1)} %get-tuple-element.777), kind=kOutput, calls=%fused_computation.95 | convolution fusion | flops 268435456 | bytes 3145728 | tf_op jit(solution)/shard_map/agnm,nagd->mad/dot_general | solution.py:54
  158.7 66.2 %reduce-scatter.5.cloned.1.call-done = bf16[2,64,512]{2,1,0:T(8,128)(2,1)} async-done(((bf16[32,64,512]{2,1,0:T(8,128)(2,1)}), bf16[2,64,512]{2,1,0:T(8,128)(2,1)}) %reduce-scatter.5.cloned.1.call-update) | async-done | bytes 131088 | tf_op jit(solution)/shard_map/reduce_scatter | solution.py:132
  (203 shorter events, 38.4 us)
Async XLA Ops:
  8.0 4.4 %copy-start = (bf16[512,576]{0,1:T(8,128)(2,1)S(1)}, bf16[512,576]{0,1:T(8,128)(2,1)}, u32[]{:S(2)}) copy-start(bf16[512,576]{0,1:T(8,128)(2,1)} %param.12) | copy-start | bytes 1769476
  8.0 51.9 %all-gather.2.cloned.1.call-start = ((), (), s32[]{:S(2)}) async-start(), calls=%async_computation.3 | async-start | bytes 2228224 | tf_op jit(solution)/shard_map/all_gather | solution.py:106
  12.3 63.4 %reduce-scatter.3.cloned.1.call-start = ((), (), s32[]{:S(2)}) async-start(), calls=%async_computation.2 | async-start | bytes 9437184 | tf_op jit(solution)/shard_map/reduce_scatter | solution.py:67
  20.5 0.9 copy-start.3
  20.5 1.0 copy-start.4
  20.5 1.8 copy-start.12
  20.5 1.9 copy-start.10
  20.6 3.2 %copy-start.9 = (bf16[512,512]{1,0:T(8,128)(2,1)S(1)}, bf16[512,512]{1,0:T(8,128)(2,1)}, u32[]{:S(2)}) copy-start(bf16[512,512]{1,0:T(8,128)(2,1)} %param.14) | copy-start | bytes 1572868
  20.6 4.4 %copy-start.11 = (s32[16]{0:T(128)S(1)}, s32[16]{0:T(128)}, u32[]{:S(2)}) copy-start(s32[16]{0:T(128)} %param.19) | copy-start | bytes 196
  20.6 204.3 %reduce-scatter.5.cloned.1.call-start = ((), (), s32[]{:S(2)}) async-start(), calls=%async_computation.4 | async-start | bytes 2228224 | tf_op jit(solution)/shard_map/reduce_scatter | solution.py:132
  77.0 6.0 %copy-start.6 = (bf16[512,512]{1,0:T(8,128)(2,1)}, bf16[512,512]{1,0:T(8,128)(2,1)S(1)}, u32[]{:S(2)}) copy-start(bf16[512,512]{1,0:T(8,128)(2,1)S(1)} %convert_element_type.56) | copy-start | bytes 1572868
  84.0 2.6 %copy-start.7 = (bf16[2,2,128,512]{3,2,1,0:T(8,128)(2,1)S(1)}, bf16[2,2,128,512]{3,2,1,0:T(8,128)(2,1)}, u32[]{:S(2)}) copy-start(bf16[2,2,128,512]{3,2,1,0:T(8,128)(2,1)} %get-tuple-element.728) | copy-start | bytes 1572868 | tf_op jit(solution)/shard_map/while
  89.2 2.6 %copy-start.7 = (bf16[2,2,128,512]{3,2,1,0:T(8,128)(2,1)S(1)}, bf16[2,2,128,512]{3,2,1,0:T(8,128)(2,1)}, u32[]{:S(2)}) copy-start(bf16[2,2,128,512]{3,2,1,0:T(8,128)(2,1)} %get-tuple-element.728) | copy-start | bytes 1572868 | tf_op jit(solution)/shard_map/while
  94.3 2.6 %copy-start.7 = (bf16[2,2,128,512]{3,2,1,0:T(8,128)(2,1)S(1)}, bf16[2,2,128,512]{3,2,1,0:T(8,128)(2,1)}, u32[]{:S(2)}) copy-start(bf16[2,2,128,512]{3,2,1,0:T(8,128)(2,1)} %get-tuple-element.728) | copy-start | bytes 1572868 | tf_op jit(solution)/shard_map/while
  99.6 2.6 %copy-start.7 = (bf16[2,2,128,512]{3,2,1,0:T(8,128)(2,1)S(1)}, bf16[2,2,128,512]{3,2,1,0:T(8,128)(2,1)}, u32[]{:S(2)}) copy-start(bf16[2,2,128,512]{3,2,1,0:T(8,128)(2,1)} %get-tuple-element.728) | copy-start | bytes 1572868 | tf_op jit(solution)/shard_map/while
  103.8 5.3 %copy-start.1 = (bf16[4,512,512]{1,2,0:T(8,128)(2,1)}, bf16[4,512,512]{1,2,0:T(8,128)(2,1)S(1)}, u32[]{:S(2)}) copy-start(bf16[4,512,512]{1,2,0:T(8,128)(2,1)S(1)} %get-tuple-element.778) | copy-start | bytes 6291460
  109.1 1.4 copy-start.2
  114.0 37.0 %copy-start.5 = (pred[512,512]{0,1:T(8,128)(4,1)S(1)}, pred[512,512]{0,1:T(8,128)(4,1)}, u32[]{:S(2)}) copy-start(pred[512,512]{0,1:T(8,128)(4,1)} %fusion.28) | copy-start | bytes 786436
  114.2 2.7 %copy-start.8 = (bf16[2,2,128,512]{3,2,1,0:T(8,128)(2,1)S(1)}, bf16[2,2,128,512]{3,2,1,0:T(8,128)(2,1)}, u32[]{:S(2)}) copy-start(bf16[2,2,128,512]{3,2,1,0:T(8,128)(2,1)} %get-tuple-element.769) | copy-start | bytes 1572868 | tf_op jit(solution)/shard_map/while
  123.4 2.7 %copy-start.8 = (bf16[2,2,128,512]{3,2,1,0:T(8,128)(2,1)S(1)}, bf16[2,2,128,512]{3,2,1,0:T(8,128)(2,1)}, u32[]{:S(2)}) copy-start(bf16[2,2,128,512]{3,2,1,0:T(8,128)(2,1)} %get-tuple-element.769) | copy-start | bytes 1572868 | tf_op jit(solution)/shard_map/while
  132.6 2.7 %copy-start.8 = (bf16[2,2,128,512]{3,2,1,0:T(8,128)(2,1)S(1)}, bf16[2,2,128,512]{3,2,1,0:T(8,128)(2,1)}, u32[]{:S(2)}) copy-start(bf16[2,2,128,512]{3,2,1,0:T(8,128)(2,1)} %get-tuple-element.769) | copy-start | bytes 1572868 | tf_op jit(solution)/shard_map/while
  141.8 2.7 %copy-start.8 = (bf16[2,2,128,512]{3,2,1,0:T(8,128)(2,1)S(1)}, bf16[2,2,128,512]{3,2,1,0:T(8,128)(2,1)}, u32[]{:S(2)}) copy-start(bf16[2,2,128,512]{3,2,1,0:T(8,128)(2,1)} %get-tuple-element.769) | copy-start | bytes 1572868 | tf_op jit(solution)/shard_map/while
Sparse Core Ops, SparseCore 0:
  12.4 47.4 all-gather.1
  151.1 73.7 reduce-scatter.4
Sparse Core Ops, SparseCore 1:
  20.7 55.0 reduce-scatter.2
where the time goes:
time: 236 us; the launch traced here: 235 us
  waiting for transfers between devices  110 us (47%)
  matrix products  67.8 us (29%)
  local copies, waits for them, and re-layouts  24.7 us (10%)
  between operations  15.8 us (7%)
  other arithmetic  15.5 us (7%)
    reduce_scatter x1, waiting for transfers between devices, shards(): lax.psum_scatter(prompt_terms.astype(jnp.bfloat16), 'seq', scatter_dimens...  66.2 us
    all_gather x1, waiting for transfers between devices, shards(): lax.all_gather(prompt_buf, 'seq', axis=0, tiled=True)  31 us
    dot_general x9, matrix products, scores(): jnp.einsum('agdn,mad->agnm', head_grad, value_part, preferred_element_typ...  22.1 us
    dot_general x9, matrix products, scores(): jnp.einsum('nagd,mad->agnm', queries, key_part, preferred_element_type=jn...  16.2 us
    reduce_scatter x1, waiting for transfers between devices, shards(): lax.psum_scatter(jnp.einsum('cd,td->ct', out_weight, out_grad, preferred_...  13 us
    dot_general x5, matrix products, grads(): jnp.einsum('agnm,agdn->mad', prob16, head_grad, preferred_element_type=jn...  9.89 us
    dot_general x1, matrix products, shards(): jnp.einsum('cd,td->ct', out_weight, out_grad, preferred_element_type=jnp....  8.16 us
    unnamed x26, local copies, waits for them, and re-layouts  7.66 us
  transfers between devices with their start and end apart: 3, of which 3 were waited for; matrix products, arithmetic and copies ran while one was open for 11% of the time, Pallas kernels for 0%

commit v1 on v0

v1 whole, which is shorter than its diff:
```python
import functools

import jax
import jax.numpy as jnp
from jax import lax
from jax.experimental import pallas as pl
from jax.experimental.pallas import tpu as pltpu
from jax.sharding import PartitionSpec as P

HD = 128
BLK = 64
BLK_DEV = 8
PCAP = 2
ROWS = BLK * BLK_DEV
PKEYS = 16 * BLK
KEYS = PKEYS + ROWS
CHUNK = 256
QB = 256

SCALE = 144.0 ** (-0.5)
SOFTCAP = 50.0

INV = 0
ORDER = 32
BASE = 40
RESP = 48
COUNT = 56
META = 64

SMEM = pltpu.MemorySpace.SMEM
VMEM = pltpu.MemorySpace.VMEM


def params(mib):
    return pltpu.CompilerParams(vmem_limit_bytes=mib * 2**20)


def layout_kernel(ids, seq, pos, depth, keys, values, meta, out):
    me = ids[0]
    for i in range(META):
        meta[i] = jnp.int32(-1)

    def device(dev, carry):
        count = jnp.int32(0)
        for b in range(BLK_DEV):
            slot = dev * BLK_DEV + b
            prompt = seq[slot] == 0

            @pl.when(prompt)
            def _(count=count, slot=slot):
                meta[INV + dev * PCAP + jnp.minimum(count, PCAP - 1)] = pos[slot]

            count = count + prompt.astype(jnp.int32)
        return carry

    lax.fori_loop(0, 16, device, 0)
    count = jnp.int32(0)
    for b in range(BLK_DEV):
        slot = me * BLK_DEV + b
        prompt = seq[slot] == 0
        at = jnp.where(prompt, BLK_DEV - 1 - count, pos[slot])
        meta[ORDER + at] = jnp.int32(b)
        meta[RESP + at] = 1 - prompt.astype(jnp.int32)
        meta[BASE + at] = jnp.where(prompt, pos[slot], depth[jnp.maximum(seq[slot] - 1, 0)]) * BLK

        @pl.when(prompt)
        def _(count=count, b=b):
            rows = pl.ds(pl.multiple_of(jnp.minimum(count, PCAP - 1) * BLK, BLK), BLK)
            out[0, rows, : keys.shape[1]] = keys[b * BLK : (b + 1) * BLK, :]
            out[0, rows, keys.shape[1] :] = values[b * BLK : (b + 1) * BLK, :]

        count = count + prompt.astype(jnp.int32)
    meta[COUNT] = count
    for b in range(PCAP):

        @pl.when(count <= b)
        def _(b=b):
            out[0, b * BLK : (b + 1) * BLK, :] = jnp.zeros((BLK, out.shape[2]), out.dtype)

    for d in range(1, 16):
        out[d] = out[0]


def layout(ids, slot_seq, slot_pos, fork_depth, keys, values):
    feat = keys.shape[1] + values.shape[1]
    return pl.pallas_call(
        layout_kernel,
        out_shape=(
            jax.ShapeDtypeStruct((META,), jnp.int32),
            jax.ShapeDtypeStruct((16, PCAP * BLK, feat), jnp.bfloat16),
        ),
        in_specs=[pl.BlockSpec(memory_space=SMEM)] * 4 + [pl.BlockSpec(memory_space=VMEM)] * 2,
        out_specs=(pl.BlockSpec(memory_space=SMEM), pl.BlockSpec(memory_space=VMEM)),
        compiler_params=params(16),
        name="layout",
    )(ids, slot_seq, slot_pos, fork_depth, keys, values)


NT = (((1,), (1,)), ((), ()))


def project_peer_kernel(ids, grad, weight, out):
    out[0] = lax.dot_general(grad[...], weight[...], NT, preferred_element_type=jnp.float32).astype(jnp.bfloat16)


def target(ids, r):
    z = ids[1]
    return jnp.where(r == 0, (3 - z) ^ 1, jnp.where(r == 1, z ^ 1, jnp.where(r == 2, 3 - z, z)))


def project_peer(ids, out_grad, out_weight):
    rows, depth = out_grad.shape
    cols = out_weight.shape[0] // 8
    return pl.pallas_call(
        project_peer_kernel,
        out_shape=jax.ShapeDtypeStruct((4, rows, cols), jnp.bfloat16),
        grid_spec=pltpu.PrefetchScalarGridSpec(
            num_scalar_prefetch=1,
            grid=(4,),
            in_specs=[
                pl.BlockSpec((rows, depth), lambda r, ids: (0, 0)),
                pl.BlockSpec((cols, depth), lambda r, ids: (target(ids, r) * 2 + 1 - ids[2], 0)),
            ],
            out_specs=pl.BlockSpec((1, rows, cols), lambda r, ids: (r, 0, 0)),
        ),
        compiler_params=params(32),
        cost_estimate=pl.CostEstimate(flops=4 * 2 * rows * cols * depth, bytes_accessed=5 * 2**20, transcendentals=0),
        name="project_peer",
    )(ids, out_grad, out_weight)


def project_own_kernel(ids, grad, weight, peer, send_a, keep_a, send_b, keep_b):
    r = pl.program_id(0)
    both = lax.dot_general(grad[...], weight[...], NT, preferred_element_type=jnp.float32)
    both = (both + peer[0].astype(jnp.float32)).astype(jnp.bfloat16)
    half = both.shape[1] // 2
    first, second = both[:, :half], both[:, half:]

    @pl.when(r < 2)
    def _():
        send_a[0] = first

    @pl.when(r >= 2)
    def _():
        keep_a[0] = first

    @pl.when(r % 2 == 0)
    def _():
        send_b[0] = second

    @pl.when(r % 2 == 1)
    def _():
        keep_b[0] = second


def project_own(ids, out_grad, out_weight, peer):
    rows, depth = out_grad.shape
    cols = out_weight.shape[0] // 8
    part = jax.ShapeDtypeStruct((2, rows, cols // 2), jnp.bfloat16)

    def at(index):
        return pl.BlockSpec((1, rows, cols // 2), lambda r, ids: (index(r), 0, 0))

    return pl.pallas_call(
        project_own_kernel,
        out_shape=(part, part, part, part),
        grid_spec=pltpu.PrefetchScalarGridSpec(
            num_scalar_prefetch=1,
            grid=(4,),
            in_specs=[
                pl.BlockSpec((rows, depth), lambda r, ids: (0, 0)),
                pl.BlockSpec((cols, depth), lambda r, ids: (target(ids, r) * 2 + ids[2], 0)),
                pl.BlockSpec((1, rows, cols), lambda r, ids: (r, 0, 0)),
            ],
            out_specs=(
                at(lambda r: jnp.where(r == 0, 1, 0)),
                at(lambda r: jnp.where(r == 3, 0, 1)),
                at(lambda r: jnp.where(r == 0, 1, 0)),
                at(lambda r: jnp.where(r >= 2, 0, 1)),
            ),
        ),
        compiler_params=params(32),
        cost_estimate=pl.CostEstimate(flops=4 * 2 * rows * cols * depth, bytes_accessed=7 * 2**20, transcendentals=0),
        name="project_own",
    )(ids, out_grad, out_weight, peer)


def attend_kernel(
    meta, q, k, v, pk, pv, ka, ra, sa, kb, rb, sb,
    dq, dk, dv, ret,
    kc, vc, kt, qc, gc, gsum, dkc, dvc, ex, fx, dp,
):
    a = pl.program_id(0)

    @pl.when(a == 0)
    def _():
        total = ka[0].astype(jnp.float32) + ra[0].astype(jnp.float32) + sa[...].astype(jnp.float32)
        gsum[...] = total.astype(jnp.bfloat16)

    @pl.when(a == 1)
    def _():
        total = kb[0].astype(jnp.float32) + rb[0].astype(jnp.float32) + sb[...].astype(jnp.float32)
        gsum[...] = total.astype(jnp.bfloat16)

    def block(i):
        return pl.ds(pl.multiple_of(i * BLK, BLK), BLK)

    for s in range(32):
        p = meta[INV + s]

        @pl.when(p >= 0)
        def _(s=s, p=p):
            kc[block(p), :] = pk[s * BLK : (s + 1) * BLK, :]
            vc[block(p), :] = pv[s * BLK : (s + 1) * BLK, :]

    lane = lax.broadcasted_iota(jnp.int32, (8, ROWS), 1)
    plim = jnp.zeros((8, ROWS), jnp.int32)
    llim = jnp.zeros((8, ROWS), jnp.int32)
    for j in range(BLK_DEV):
        src = block(meta[ORDER + j])
        kc[PKEYS + j * BLK : PKEYS + (j + 1) * BLK, :] = k[src, :]
        vc[PKEYS + j * BLK : PKEYS + (j + 1) * BLK, :] = v[src, :]
        for h in range(2):
            to = slice(h * ROWS + j * BLK, h * ROWS + (j + 1) * BLK)
            qc[to, :] = q[src, h * HD : (h + 1) * HD]
            gc[to, :] = gsum[src, h * HD : (h + 1) * HD]
        here = (lane >= j * BLK) & (lane < (j + 1) * BLK)
        resp = meta[RESP + j]
        step = lane - (j * BLK - 1)
        plim = jnp.where(here, meta[BASE + j] + step * (1 - resp), plim)
        llim = jnp.where(here, (j * BLK + step) * resp, llim)
    kt[...] = kc[...].T
    sub = lax.broadcasted_iota(jnp.int32, (CHUNK, QB), 0)

    for h in range(2):
        for half in range(ROWS // QB):
            rows = slice(h * ROWS + half * QB, h * ROWS + (half + 1) * QB)
            qb = qc[rows, :]
            gb = gc[rows, :]
            lanes = slice(half * QB, (half + 1) * QB)
            pl_row = plim[:1, lanes]
            ll_row = llim[:1, lanes]
            chunks = PKEYS // CHUNK + half + 1
            total = jnp.zeros((1, QB), jnp.float32)
            weighted = jnp.zeros((1, QB), jnp.float32)
            for c in range(chunks):
                cut = slice(c * CHUNK, (c + 1) * CHUNK)
                raw = lax.dot_general(kc[cut, :], qb, NT, preferred_element_type=jnp.float32)
                dprob = lax.dot_general(vc[cut, :], gb, NT, preferred_element_type=jnp.float32)
                tanh_val = jnp.tanh(raw * (SCALE / SOFTCAP))
                if c * CHUNK < PKEYS:
                    seen = sub < pl_row - c * CHUNK
                else:
                    seen = sub < ll_row - (c * CHUNK - PKEYS)
                expo = jnp.where(seen, jnp.exp(SOFTCAP * tanh_val), 0.0)
                total = total + jnp.sum(expo, axis=0, keepdims=True)
                weighted = weighted + jnp.sum(expo * dprob, axis=0, keepdims=True)
                ex[cut, :] = expo
                fx[cut, :] = expo * (1.0 - tanh_val * tanh_val)
                dp[cut, :] = dprob
            inv = 1.0 / total
            delta = weighted * inv
            scaled = inv * SCALE
            dq_t = jnp.zeros((HD, QB), jnp.float32)
            for c in range(chunks):
                cut = slice(c * CHUNK, (c + 1) * CHUNK)
                prob16 = (ex[cut, :] * inv).astype(jnp.bfloat16)
                dscore16 = (fx[cut, :] * ((dp[cut, :] - delta) * scaled)).astype(jnp.bfloat16)
                dv_part = jnp.dot(prob16, gb, preferred_element_type=jnp.float32)
                dk_part = jnp.dot(dscore16, qb, preferred_element_type=jnp.float32)
                dq_t = dq_t + jnp.dot(kt[:, cut], dscore16, preferred_element_type=jnp.float32)
                first = h == 0 and (half == 0 or c == PKEYS // CHUNK + 1)
                if first:
                    dvc[cut, :] = dv_part
                    dkc[cut, :] = dk_part
                else:
                    dvc[cut, :] += dv_part
                    dkc[cut, :] += dk_part
            dq_rows = dq_t.T.astype(jnp.bfloat16)
            for j in range(QB // BLK):
                dst = block(meta[ORDER + half * (QB // BLK) + j])
                dq[dst, h * HD : (h + 1) * HD] = dq_rows[j * BLK : (j + 1) * BLK, :]

    for j in range(BLK_DEV):
        dst = block(meta[ORDER + j])
        src = slice(PKEYS + j * BLK, PKEYS + (j + 1) * BLK)
        dk[dst, :] = dkc[src, :].astype(jnp.bfloat16)
        dv[dst, :] = dvc[src, :].astype(jnp.bfloat16)
    for s in range(32):
        p = meta[INV + s]
        to = slice((s % 2) * BLK, (s % 2 + 1) * BLK)

        @pl.when(p >= 0)
        def _(s=s, p=p, to=to):
            ret[s // 2, to, :HD] = dkc[block(p), :].astype(jnp.bfloat16)
            ret[s // 2, to, HD:] = dvc[block(p), :].astype(jnp.bfloat16)

        @pl.when(p < 0)
        def _(s=s, to=to):
            ret[s // 2, to, :] = jnp.zeros((BLK, 2 * HD), jnp.bfloat16)


def attend(meta, queries, keys, values, gathered, parts):
    full = pl.BlockSpec((ROWS, 2 * HD), lambda a: (0, 0))
    first = pl.BlockSpec((1, ROWS, 2 * HD), lambda a: (0, 0, 0))
    wide = pl.BlockSpec((ROWS, 2 * HD), lambda a: (0, a))
    narrow = pl.BlockSpec((ROWS, HD), lambda a: (0, a))
    slots = 16 * PCAP * BLK
    return pl.pallas_call(
        attend_kernel,
        out_shape=(
            jax.ShapeDtypeStruct(queries.shape, jnp.bfloat16),
            jax.ShapeDtypeStruct(keys.shape, jnp.bfloat16),
            jax.ShapeDtypeStruct(values.shape, jnp.bfloat16),
            jax.ShapeDtypeStruct((16, PCAP * BLK, 4 * HD), jnp.bfloat16),
        ),
        grid=(2,),
        in_specs=[
            pl.BlockSpec(memory_space=SMEM),
            wide,
            narrow,
            narrow,
            pl.BlockSpec((slots, HD), lambda a: (0, a)),
            pl.BlockSpec((slots, HD), lambda a: (0, 2 + a)),
            first, first, full, first, first, full,
        ],
        out_specs=(wide, narrow, narrow, pl.BlockSpec((16, PCAP * BLK, 2 * HD), lambda a: (0, 0, a))),
        scratch_shapes=[
            pltpu.VMEM((KEYS, HD), jnp.bfloat16),
            pltpu.VMEM((KEYS, HD), jnp.bfloat16),
            pltpu.VMEM((HD, KEYS), jnp.bfloat16),
            pltpu.VMEM((2 * ROWS, HD), jnp.bfloat16),
            pltpu.VMEM((2 * ROWS, HD), jnp.bfloat16),
            pltpu.VMEM((ROWS, 2 * HD), jnp.bfloat16),
            pltpu.VMEM((KEYS, HD), jnp.float32),
            pltpu.VMEM((KEYS, HD), jnp.float32),
            pltpu.VMEM((KEYS, QB), jnp.float32),
            pltpu.VMEM((KEYS, QB), jnp.float32),
            pltpu.VMEM((KEYS, QB), jnp.float32),
        ],
        compiler_params=params(48),
        cost_estimate=pl.CostEstimate(flops=4 * 10**9, bytes_accessed=8 * 2**20, transcendentals=6 * 10**6),
        name="attend",
    )(meta, queries, keys, values, gathered, gathered, *parts)


def finish_kernel(meta, ret, dk_in, dv_in, dk, dv):
    dk[...] = dk_in[...]
    dv[...] = dv_in[...]
    for r in range(PCAP):

        @pl.when(meta[COUNT] > r)
        def _(r=r):
            rows = slice(r * BLK, (r + 1) * BLK)
            at = pl.ds(pl.multiple_of(meta[ORDER + BLK_DEV - 1 - r] * BLK, BLK), BLK)
            for a in range(2):
                for i, out in enumerate((dk, dv)):
                    cols = slice((2 * a + i) * HD, (2 * a + i + 1) * HD)
                    total = ret[0, rows, cols].astype(jnp.float32)
                    for d in range(1, 16):
                        total = total + ret[d, rows, cols].astype(jnp.float32)
                    out[at, a * HD : (a + 1) * HD] = total.astype(jnp.bfloat16)


def finish(meta, ret, dk, dv):
    return pl.pallas_call(
        finish_kernel,
        out_shape=(jax.ShapeDtypeStruct(dk.shape, dk.dtype), jax.ShapeDtypeStruct(dv.shape, dv.dtype)),
        in_specs=[pl.BlockSpec(memory_space=SMEM)] + [pl.BlockSpec(memory_space=VMEM)] * 3,
        out_specs=(pl.BlockSpec(memory_space=VMEM), pl.BlockSpec(memory_space=VMEM)),
        compiler_params=params(16),
        name="finish",
    )(meta, ret, dk, dv)


def shards(out_grad, out_weight, query_states, key_states, value_states, slot_seq, slot_pos, fork_depth):
    ids = jnp.stack([lax.axis_index("seq"), lax.axis_index("mp"), lax.axis_index("section")]).astype(jnp.int32)
    pair_a = [(z, z ^ 1) for z in range(4)]
    pair_b = [(z, 3 - z) for z in range(4)]
    swap = [(0, 1), (1, 0)]

    peer = project_peer(ids, out_grad, out_weight)
    peer = lax.ppermute(peer, "section", swap)
    meta, prompt = layout(ids, slot_seq, slot_pos, fork_depth, key_states, value_states)
    gathered = lax.all_to_all(prompt, "seq", 0, 0, tiled=True).reshape(16 * PCAP * BLK, -1)
    send_a, keep_a, send_b, keep_b = project_own(ids, out_grad, out_weight, peer)
    recv_a = lax.ppermute(send_a, "mp", pair_a)
    recv_b = lax.ppermute(send_b, "mp", pair_b)
    next_a = (keep_a[1].astype(jnp.float32) + recv_a[1].astype(jnp.float32)).astype(jnp.bfloat16)
    next_b = (keep_b[1].astype(jnp.float32) + recv_b[1].astype(jnp.float32)).astype(jnp.bfloat16)
    last_a = lax.ppermute(next_a, "mp", pair_b)
    last_b = lax.ppermute(next_b, "mp", pair_a)
    parts = (keep_a, recv_a, last_a, keep_b, recv_b, last_b)
    dq, dk, dv, ret = attend(meta, query_states, key_states, value_states, gathered, parts)
    ret = lax.all_to_all(ret, "seq", 0, 0, tiled=True)
    dk, dv = finish(meta, ret, dk, dv)
    return dq, dk, dv


def solution(mesh):
    wide = P("seq", ("mp", "section"))
    return jax.shard_map(
        shards,
        mesh=mesh,
        in_specs=(wide, P(None, ("mp", "section")), wide, wide, wide, P(), P(), P()),
        out_specs=(wide, wide, wide),
        check_vma=False,
    )
```

time: 236 us -> 114 us (0.48)
  waiting for transfers between devices: 110 us -> 22.3 us
  matrix products: 67.8 us -> 0 us
  blocking collectives: 0 us -> 32.9 us
  Pallas kernels: 0 us -> 28.2 us
  other arithmetic: 15.5 us -> 0.21 us
  between operations: 15.8 us -> 0.78 us
  starting transfers between devices: 0.3 us -> 13.1 us
  local copies, waits for them, and re-layouts: 24.7 us -> 16.1 us
    reduce_scatter x2 -> x0, waiting for transfers between devices: 79.2 us -> none  [the longest x1 66.2 us: shards(): lax.psum_scatter(prompt_terms.astype(jnp.bfloat16), 'seq', scatter_dimens...]
    dot_general x36 -> x0, matrix products: 67.8 us -> none  [the longest x9 22.1 us: scores(): jnp.einsum('agdn,mad->agnm', head_grad, value_part, preferred_element_typ...]
    all_to_all x0 -> x1, blocking collectives: none -> 32.9 us  [shards(): ret = lax.all_to_all(ret, 'seq', 0, 0, tiled=True)]
    all_gather x1 -> x0, waiting for transfers between devices: 31 us -> none  [shards(): lax.all_gather(prompt_buf, 'seq', axis=0, tiled=True)]
    pallas_call x0 -> x5, Pallas kernels: none -> 28.2 us  [the longest x1 16.5 us: attend(): pl.pallas_call(attend_kernel, out_shape=(jax.ShapeDtypeStruct(queries.sha...]
    ppermute x0 -> x5, waiting for transfers between devices: none -> 13.6 us  [the longest x1 12.3 us: shards(): recv_b = lax.ppermute(send_b, 'mp', pair_b)]
    all_to_all x0 -> x1, waiting for transfers between devices: none -> 8.68 us  [shards(): lax.all_to_all(prompt, 'seq', 0, 0, tiled=True).reshape(16 * PCAP * BLK, -1)]
    unnamed x26 -> x28, local copies, waits for them, and re-layouts: 7.66 us -> 16.1 us
  transfers between devices with their start and end apart: 3 -> 6, of which waited for: 3 -> 3; matrix products, arithmetic and copies ran while one was open for 11% -> 0% of each run, Pallas kernels for 0% -> 5%
where the time goes in v1:
time: 114 us
  blocking collectives  32.9 us (29%)
  Pallas kernels  28.2 us (25%)
  waiting for transfers between devices  22.3 us (20%)
  local copies, waits for them, and re-layouts  16.1 us (14%)
  starting transfers between devices  13.1 us (11%)
    all_to_all x1, blocking collectives, shards(): ret = lax.all_to_all(ret, 'seq', 0, 0, tiled=True)  32.9 us
    pallas_call x1, Pallas kernels, attend(): pl.pallas_call(attend_kernel, out_shape=(jax.ShapeDtypeStruct(queries.sha...  16.5 us
    unnamed x28, local copies, waits for them, and re-layouts  16.1 us
    ppermute x1, waiting for transfers between devices, shards(): recv_b = lax.ppermute(send_b, 'mp', pair_b)  12.3 us
    all_to_all x1, waiting for transfers between devices, shards(): lax.all_to_all(prompt, 'seq', 0, 0, tiled=True).reshape(16 * PCAP * BLK, -1)  8.68 us
    all_to_all x1, starting transfers between devices, shards(): lax.all_to_all(prompt, 'seq', 0, 0, tiled=True).reshape(16 * PCAP * BLK, -1)  7.18 us
    ppermute x1, starting transfers between devices, shards(): recv_b = lax.ppermute(send_b, 'mp', pair_b)  4.12 us
    pallas_call x1, Pallas kernels, project_peer(): pl.pallas_call(project_peer_kernel, out_shape=jax.ShapeDtypeStruct((4, ro...  4.03 us
  transfers between devices with their start and end apart: 6, of which 3 were waited for; matrix products, arithmetic and copies ran while one was open for 0% of the time, Pallas kernels for 5%

profile of v1, /device:TPU:0, one launch (start us, length us, event | category | flops | bytes accessed | tf_op | source)
XLA Modules:
  0.0 113.7 jit_solution(13362061761712425976)
XLA Ops:
  0.6 7.7 %copy.14.weight = bf16[4096,576]{1,0:T(8,128)(2,1)} copy(bf16[4096,576]{0,1:T(8,128)(2,1)} %param.9) | data formatting | bytes 9437184 | tf_op args[1]
  8.3 0.3 copy.13.grad
  8.6 0.1 pad_add_fusion.ids
  8.7 2.5 %copy-done = bf16[4096,576]{1,0:T(8,128)(2,1)S(1)} copy-done((bf16[4096,576]{1,0:T(8,128)(2,1)S(1)}, bf16[4096,576]{1,0:T(8,128)(2,1)}, u32[]{:S(2)}) %copy-start) | copy-done | bytes 4718616
  11.2 0.0 copy-start.10
  11.2 4.0 %project_peer.1 = bf16[4,512,512]{2,1,0:T(8,128)(2,1)} custom-call(s32[3]{0:T(128)S(1)} %pad_add_fusion.ids, bf16[512,576]{1,0:T(8,128)(2,1)S(1)} %copy.13.grad, bf16[4096,576]{1,0:T(8,128)(2,1)S(1)} %copy-done), custom_call_target="tpu_custom_call" | custom-call | flops 1207959552 | bytes 5242880 | tf_op jit(solution)/shard_map/project_peer/pallas_call | solution.py:114
  15.3 0.0 collective-permute-start
  15.3 0.0 copy-done.3
  15.3 2.8 %layout.1 = (s32[64]{0:T(128)S(1)}, bf16[16,128,512]{2,1,0:T(8,128)(2,1)}) custom-call(s32[3]{0:T(128)S(1)} %pad_add_fusion.ids, s32[128]{0:T(128)S(1)} %copy-done.8, s32[128]{0:T(128)S(1)} %copy-done.9, s32[16]{0:T(128)S(1)} %copy-done.10, bf16[512,256]{1,0:T(8,128)(2,1)S(1)} %copy-done.2, bf16[512,256]{1,0:T(8,128)(2,1)S(1)} %copy-done.3), custom_call_target="tpu_custom_call" | custom-call | tf_op jit(solution)/shard_map/layout/pallas_call | solution.py:86
  18.1 7.2 %all-to-all-start = ((bf16[16,128,512]{2,1,0:T(8,128)(2,1)}), bf16[16,128,512]{2,1,0:T(8,128)(2,1)}, u32[]{:S(2)}, u32[]{:S(2)}) async-start(bf16[16,128,512]{2,1,0:T(8,128)(2,1)} %get-tuple-element.16), calls=%async_computation | async-start | bytes 4194304 | tf_op jit(solution)/shard_map/all_to_all | solution.py:385
  25.3 0.0 collective-permute-done.peer
  25.3 0.0 copy-start.1
  25.3 2.5 %copy-done.1 = bf16[4096,576]{1,0:T(8,128)(2,1)S(1)} copy-done((bf16[4096,576]{1,0:T(8,128)(2,1)S(1)}, bf16[4096,576]{1,0:T(8,128)(2,1)}, u32[]{:S(2)}) %copy-start.1) | copy-done | bytes 4718616
  27.8 3.3 %project_own.1 = (bf16[2,512,256]{2,1,0:T(8,128)(2,1)S(1)}, bf16[2,512,256]{2,1,0:T(8,128)(2,1)S(1)}, bf16[2,512,256]{2,1,0:T(8,128)(2,1)S(1)}, bf16[2,512,256]{2,1,0:T(8,128)(2,1)S(1)}) custom-call(s32[3]{0:T(128)S(1)} %pad_add_fusion.ids, bf16[512,576]{1,0:T(8,128)(2,1)S(1)} %copy.13.grad, bf16[4096,576]{1,0:T(8,128)(2,1)S(1)} %copy-done.1, ...), custom_call_target="tpu_custom_call" | custom-call | flops 1207959552 | bytes 7340032 | tf_op jit(solution)/shard_map/project_own/pallas_call | solution.py:164
  31.1 0.0 copy-start.4
  31.2 4.1 %collective-permute-start.3 = (bf16[2,512,256]{2,1,0:T(8,128)(2,1)S(1)}, bf16[2,512,256]{2,1,0:T(8,128)(2,1)S(1)}, u32[]{:S(2)}, u32[]{:S(2)}) collective-permute-start(bf16[2,512,256]{2,1,0:T(8,128)(2,1)S(1)} %get-tuple-element.20), channel_id=1, source_target_pairs={{0,6},{2,4},{4,2},{6,0},{1,7},{3,5},{5,3},{7,1},{8,14},{10,12},{12... | collective-permute-start | bytes 1572872 | tf_op jit(solution)/shard_map/ppermute | solution.py:388
  35.3 0.0 collective-permute-start.1
  35.3 12.3 %collective-permute-done.3.rb = bf16[2,512,256]{2,1,0:T(8,128)(2,1)S(1)} collective-permute-done((bf16[2,512,256]{2,1,0:T(8,128)(2,1)S(1)}, bf16[2,512,256]{2,1,0:T(8,128)(2,1)S(1)}, u32[]{:S(2)}, u32[]{:S(2)}) %collective-permute-start.3) | collective-permute-done | bytes 524320 | tf_op jit(solution)/shard_map/ppermute | solution.py:388
  47.6 0.1 fusion.1
  47.7 0.1 collective-permute-start.4
  47.7 1.3 %collective-permute-done.1.ra = bf16[2,512,256]{2,1,0:T(8,128)(2,1)S(1)} collective-permute-done((bf16[2,512,256]{2,1,0:T(8,128)(2,1)S(1)}, bf16[2,512,256]{2,1,0:T(8,128)(2,1)S(1)}, u32[]{:S(2)}, u32[]{:S(2)}) %collective-permute-start.1) | collective-permute-done | bytes 524320 | tf_op jit(solution)/shard_map/ppermute | solution.py:387
  49.0 0.1 fusion
  49.1 1.8 %collective-permute-start.2 = (bf16[512,256]{1,0:T(8,128)(2,1)S(1)}, bf16[512,256]{1,0:T(8,128)(2,1)S(1)}, u32[]{:S(2)}, u32[]{:S(2)}) collective-permute-start(bf16[512,256]{1,0:T(8,128)(2,1)S(1)} %fusion), channel_id=1, source_target_pairs={{0,6},{2,4},{4,2},{6,0},{1,7},{3,5},{5,3},{7,1},{8,14},{10,12},{12... | collective-permute-start | bytes 786440 | tf_op jit(solution)/shard_map/ppermute | solution.py:391
  50.9 8.7 %all-to-all-done = bf16[16,128,512]{2,1,0:T(8,128)(2,1)} async-done(((bf16[16,128,512]{2,1,0:T(8,128)(2,1)}), bf16[16,128,512]{2,1,0:T(8,128)(2,1)}, u32[]{:S(2)}, u32[]{:S(2)}) %all-to-all-start) | async-done | bytes 2097184 | tf_op jit(solution)/shard_map/all_to_all | solution.py:385
  59.6 0.0 collective-permute-done.4.sb
  59.6 0.0 collective-permute-done.2.sa
  59.6 1.0 copy-done.5
  60.6 1.0 copy-done.7
  61.7 1.0 copy-done.11
  62.7 16.5 %attend.1 = (bf16[512,512]{1,0:T(8,128)(2,1)}, bf16[512,256]{1,0:T(8,128)(2,1)S(1)}, bf16[512,256]{1,0:T(8,128)(2,1)S(1)}, bf16[16,128,512]{2,1,0:T(8,128)(2,1)}) custom-call(s32[64]{0:T(128)S(1)} %get-tuple-element.15.meta, bf16[512,512]{1,0:T(8,128)(2,1)S(1)} %copy-done.11, bf16[512,256]{1,0:T(8,128)(2,1)S(1)} %copy-done.2, ...), custom_call_target="tpu_custom_call" | custom-call | flops 4000000000 | bytes 8388608 | tf_op jit(solution)/shard_map/attend/pallas_call | solution.py:309
  79.2 32.9 %all_to_all.10.ret = bf16[16,128,512]{2,1,0:T(8,128)(2,1)S(1)} all-to-all(bf16[16,128,512]{2,1,0:T(8,128)(2,1)} %get-tuple-element.22), channel_id=1, replica_groups=mesh['seq'=16,'mp'=4,'section'=2] {'seq'}, dimensions={0} | all-to-all | bytes 4194304 | tf_op jit(solution)/shard_map/all_to_all | solution.py:395
  112.2 1.5 %finish.1 = (bf16[512,256]{1,0:T(8,128)(2,1)}, bf16[512,256]{1,0:T(8,128)(2,1)}) custom-call(s32[64]{0:T(128)S(1)} %get-tuple-element.15.meta, bf16[16,128,512]{2,1,0:T(8,128)(2,1)S(1)} %all_to_all.10.ret, bf16[512,256]{1,0:T(8,128)(2,1)S(1)} %get-tuple-element.23.dk_in, bf16[512,256]{1,0:T(8,128)(2,1)S(1)} %get-tuple-element.24.dv_in), custom_call_target="tpu_custom_call" | custom-call | tf_op jit(solution)/shard_map/finish/pallas_call | solution.py:366
  (17 shorter events, 0.0 us)
Async XLA Ops:
  0.6 7.7 %copy-start.12 = (bf16[512,576]{0,1:T(8,128)(2,1)S(1)}, bf16[512,576]{0,1:T(8,128)(2,1)}, u32[]{:S(2)}) copy-start(bf16[512,576]{0,1:T(8,128)(2,1)} %param.8) | copy-start | bytes 1769476
  8.7 2.5 %copy-start = (bf16[4096,576]{1,0:T(8,128)(2,1)S(1)}, bf16[4096,576]{1,0:T(8,128)(2,1)}, u32[]{:S(2)}) copy-start(bf16[4096,576]{1,0:T(8,128)(2,1)} %copy.14.weight) | copy-start | bytes 14155780
  11.2 4.1 %copy-start.2 = (bf16[512,256]{1,0:T(8,128)(2,1)S(1)}, bf16[512,256]{1,0:T(8,128)(2,1)}, u32[]{:S(2)}) copy-start(bf16[512,256]{1,0:T(8,128)(2,1)} %k.1) | copy-start | bytes 786436
  11.2 4.1 %copy-start.3 = (bf16[512,256]{1,0:T(8,128)(2,1)S(1)}, bf16[512,256]{1,0:T(8,128)(2,1)}, u32[]{:S(2)}) copy-start(bf16[512,256]{1,0:T(8,128)(2,1)} %v.1) | copy-start | bytes 786436
  11.2 4.1 %copy-start.8 = (s32[128]{0:T(128)S(1)}, s32[128]{0:T(128)}, u32[]{:S(2)}) copy-start(s32[128]{0:T(128)} %seq.1) | copy-start | bytes 1540
  11.2 4.1 %copy-start.9 = (s32[128]{0:T(128)S(1)}, s32[128]{0:T(128)}, u32[]{:S(2)}) copy-start(s32[128]{0:T(128)} %pos.1) | copy-start | bytes 1540
  11.2 4.1 %copy-start.10 = (s32[16]{0:T(128)S(1)}, s32[16]{0:T(128)}, u32[]{:S(2)}) copy-start(s32[16]{0:T(128)} %depth.1) | copy-start | bytes 196
  15.3 10.1 %collective-permute-start = (bf16[4,512,512]{2,1,0:T(8,128)(2,1)}, bf16[4,512,512]{2,1,0:T(8,128)(2,1)S(1)}, u32[]{:S(2)}, u32[]{:S(2)}) collective-permute-start(bf16[4,512,512]{2,1,0:T(8,128)(2,1)} %project_peer.1), channel_id=1, source_target_pairs={{0,1},{1,0},{2,3},{3,2},{4,5},{5,4},{6,7},{7,6},{8,9},{9,8},{10,11... | collective-permute-start | bytes 6291464 | tf_op jit(solution)/shard_map/ppermute | solution.py:383
  18.1 41.4 %all-to-all-start = ((bf16[16,128,512]{2,1,0:T(8,128)(2,1)}), bf16[16,128,512]{2,1,0:T(8,128)(2,1)}, u32[]{:S(2)}, u32[]{:S(2)}) async-start(bf16[16,128,512]{2,1,0:T(8,128)(2,1)} %get-tuple-element.16), calls=%async_computation | async-start | bytes 4194304 | tf_op jit(solution)/shard_map/all_to_all | solution.py:385
  25.3 2.5 %copy-start.1 = (bf16[4096,576]{1,0:T(8,128)(2,1)S(1)}, bf16[4096,576]{1,0:T(8,128)(2,1)}, u32[]{:S(2)}) copy-start(bf16[4096,576]{1,0:T(8,128)(2,1)} %copy.14.weight) | copy-start | bytes 14155780
  31.1 17.9 %copy-start.4 = (bf16[2,512,256]{2,1,0:T(8,128)(2,1)}, bf16[2,512,256]{2,1,0:T(8,128)(2,1)S(1)}, u32[]{:S(2)}) copy-start(bf16[2,512,256]{2,1,0:T(8,128)(2,1)S(1)} %get-tuple-element.17.ka) | copy-start | bytes 1572868
  31.2 18.0 %copy-start.6 = (bf16[2,512,256]{2,1,0:T(8,128)(2,1)}, bf16[2,512,256]{2,1,0:T(8,128)(2,1)S(1)}, u32[]{:S(2)}) copy-start(bf16[2,512,256]{2,1,0:T(8,128)(2,1)S(1)} %get-tuple-element.19.kb) | copy-start | bytes 1572868
  31.2 16.4 %collective-permute-start.3 = (bf16[2,512,256]{2,1,0:T(8,128)(2,1)S(1)}, bf16[2,512,256]{2,1,0:T(8,128)(2,1)S(1)}, u32[]{:S(2)}, u32[]{:S(2)}) collective-permute-start(bf16[2,512,256]{2,1,0:T(8,128)(2,1)S(1)} %get-tuple-element.20), channel_id=1, source_target_pairs={{0,6},{2,4},{4,2},{6,0},{1,7},{3,5},{5,3},{7,1},{8,14},{10,12},{12... | collective-permute-start | bytes 1572872 | tf_op jit(solution)/shard_map/ppermute | solution.py:388
  35.3 13.8 %collective-permute-start.1 = (bf16[2,512,256]{2,1,0:T(8,128)(2,1)S(1)}, bf16[2,512,256]{2,1,0:T(8,128)(2,1)S(1)}, u32[]{:S(2)}, u32[]{:S(2)}) collective-permute-start(bf16[2,512,256]{2,1,0:T(8,128)(2,1)S(1)} %get-tuple-element.18), channel_id=1, source_target_pairs={{0,2},{2,0},{4,6},{6,4},{1,3},{3,1},{5,7},{7,5},{8,10},{10,8},{12,... | collective-permute-start | bytes 1572872 | tf_op jit(solution)/shard_map/ppermute | solution.py:387
  47.7 11.9 %collective-permute-start.4 = (bf16[512,256]{1,0:T(8,128)(2,1)S(1)}, bf16[512,256]{1,0:T(8,128)(2,1)S(1)}, u32[]{:S(2)}, u32[]{:S(2)}) collective-permute-start(bf16[512,256]{1,0:T(8,128)(2,1)S(1)} %fusion.1), channel_id=1, source_target_pairs={{0,2},{2,0},{4,6},{6,4},{1,3},{3,1},{5,7},{7,5},{8,10},{10,8},{12,... | collective-permute-start | bytes 786440 | tf_op jit(solution)/shard_map/ppermute | solution.py:392
  49.1 10.4 %collective-permute-start.2 = (bf16[512,256]{1,0:T(8,128)(2,1)S(1)}, bf16[512,256]{1,0:T(8,128)(2,1)S(1)}, u32[]{:S(2)}, u32[]{:S(2)}) collective-permute-start(bf16[512,256]{1,0:T(8,128)(2,1)S(1)} %fusion), channel_id=1, source_target_pairs={{0,6},{2,4},{4,2},{6,0},{1,7},{3,5},{5,3},{7,1},{8,14},{10,12},{12... | collective-permute-start | bytes 786440 | tf_op jit(solution)/shard_map/ppermute | solution.py:391
  59.6 1.0 copy-start.5
  60.6 1.0 copy-start.7
  61.7 1.0 copy-start.11

commit v2 on v1

v2 whole, which is shorter than its diff:
```python
import jax
import jax.numpy as jnp
from jax import lax
from jax.experimental import pallas as pl
from jax.experimental.pallas import tpu as pltpu
from jax.sharding import PartitionSpec as P

HD = 128
BLK = 64
BLK_DEV = 8
PCAP = 2
DEVS = 16
ROWS = BLK * BLK_DEV
PKEYS = 16 * BLK
KEYS = PKEYS + ROWS
CHUNK = 256

SCALE = 144.0 ** (-0.5)
SOFTCAP = 50.0

PLIST = 0
ORDER = 16
BASE = 24
RESP = 32
COUNT = 40
META = 48

LIM = 60

SMEM = pltpu.MemorySpace.SMEM
VMEM = pltpu.MemorySpace.VMEM
NT = (((1,), (1,)), ((), ()))
TN = (((0,), (0,)), ((), ()))


def params(mib):
    return pltpu.CompilerParams(vmem_limit_bytes=mib * 2**20)


def specs(space, n):
    return [pl.BlockSpec(memory_space=space)] * n


def rows_at(i):
    return pl.ds(pl.multiple_of(i * BLK, BLK), BLK)


def place(slot):
    return lax.shift_right_logical(slot, 1), rows_at(slot & 1)


def make_layout(here, seq, pos, depth, keys, values, meta, block):
    me = here[0]

    def device(dev, carry):
        count = jnp.int32(0)
        for b in range(BLK_DEV):
            slot = dev * BLK_DEV + b
            prompt = seq[slot] == 0

            @pl.when(prompt)
            def _(count=count, slot=slot):
                meta[PLIST + pos[slot]] = dev * PCAP + jnp.minimum(count, PCAP - 1)

            count = count + prompt.astype(jnp.int32)
        return carry

    lax.fori_loop(0, DEVS, device, 0)
    count = jnp.int32(0)
    block[...] = jnp.zeros(block.shape, block.dtype)
    for b in range(BLK_DEV):
        slot = me * BLK_DEV + b
        prompt = seq[slot] == 0
        at = jnp.where(prompt, BLK_DEV - 1 - count, pos[slot])
        meta[ORDER + at] = jnp.int32(b)
        meta[RESP + at] = 1 - prompt.astype(jnp.int32)
        meta[BASE + at] = jnp.where(prompt, pos[slot], depth[jnp.maximum(seq[slot] - 1, 0)]) * BLK

        @pl.when(prompt)
        def _(count=count, b=b):
            rows = rows_at(jnp.minimum(count, PCAP - 1))
            for a in range(2):
                block[a, rows, :HD] = keys[b * BLK : (b + 1) * BLK, a * HD : (a + 1) * HD]
                block[a, rows, HD:] = values[b * BLK : (b + 1) * BLK, a * HD : (a + 1) * HD]

        count = count + prompt.astype(jnp.int32)
    meta[COUNT] = count


def target(z, r):
    z = z[0]
    return jnp.where(r == 0, (3 - z) ^ 1, jnp.where(r == 1, z ^ 1, jnp.where(r == 2, 3 - z, z)))


def project_peer_kernel(z, c, here, grad, weight, seq, pos, depth, keys, values, out, meta, prompt, block, sems):
    r = pl.program_id(0)
    copies = [pltpu.make_async_copy(block, prompt.at[d], sems.at[d]) for d in range(DEVS)]

    @pl.when(r == 0)
    def _():
        make_layout(here, seq, pos, depth, keys, values, meta, block)
        for copy in copies:
            copy.start()

    out[0] = lax.dot_general(grad[...], weight[...], TN, preferred_element_type=jnp.float32).astype(jnp.bfloat16)

    @pl.when(r == 3)
    def _():
        for copy in copies:
            copy.wait()


def project_peer(z, c, here, out_grad, out_weight, slot_seq, slot_pos, fork_depth, keys, values):
    depth, rows = out_grad.shape
    cols = out_weight.shape[1] // 8
    block = (2, PCAP * BLK, 2 * HD)
    return pl.pallas_call(
        project_peer_kernel,
        out_shape=(
            jax.ShapeDtypeStruct((4, rows, cols), jnp.bfloat16),
            jax.ShapeDtypeStruct((META,), jnp.int32),
            jax.ShapeDtypeStruct((DEVS, *block), jnp.bfloat16),
        ),
        grid_spec=pltpu.PrefetchScalarGridSpec(
            num_scalar_prefetch=3,
            grid=(4,),
            in_specs=[
                pl.BlockSpec((depth, rows), lambda r, z, c, here: (0, 0)),
                pl.BlockSpec((depth, cols), lambda r, z, c, here: (0, target(z, r) * 2 + 1 - c[0])),
                *specs(SMEM, 3),
                pl.BlockSpec(keys.shape, lambda r, z, c, here: (0, 0)),
                pl.BlockSpec(values.shape, lambda r, z, c, here: (0, 0)),
            ],
            out_specs=(
                pl.BlockSpec((1, rows, cols), lambda r, z, c, here: (r, 0, 0)),
                pl.BlockSpec(memory_space=SMEM),
                pl.BlockSpec(memory_space=pl.ANY),
            ),
            scratch_shapes=[pltpu.VMEM(block, jnp.bfloat16), pltpu.SemaphoreType.DMA((DEVS,))],
        ),
        compiler_params=params(LIM),
        cost_estimate=pl.CostEstimate(flops=4 * 2 * rows * cols * depth, bytes_accessed=5 * 2**20, transcendentals=0),
        name="project_peer",
    )(z, c, here, out_grad, out_weight, slot_seq, slot_pos, fork_depth, keys, values)


def project_own_kernel(z, c, grad, weight, peer, send_a, keep_a, send_b, keep_b):
    r = pl.program_id(0)
    both = lax.dot_general(grad[...], weight[...], TN, preferred_element_type=jnp.float32)
    both = (both + peer[0].astype(jnp.float32)).astype(jnp.bfloat16)
    half = both.shape[1] // 2
    first, second = both[:, :half], both[:, half:]

    @pl.when(r < 2)
    def _():
        send_a[0] = first

    @pl.when(r >= 2)
    def _():
        keep_a[0] = first

    @pl.when(r % 2 == 0)
    def _():
        send_b[0] = second

    @pl.when(r % 2 == 1)
    def _():
        keep_b[0] = second


def project_own(z, c, out_grad, out_weight, peer):
    depth, rows = out_grad.shape
    cols = out_weight.shape[1] // 8
    part = jax.ShapeDtypeStruct((2, rows, cols // 2), jnp.bfloat16)

    def at(index):
        return pl.BlockSpec((1, rows, cols // 2), lambda r, z, c: (index(r), 0, 0))

    return pl.pallas_call(
        project_own_kernel,
        out_shape=(part, part, part, part),
        grid_spec=pltpu.PrefetchScalarGridSpec(
            num_scalar_prefetch=2,
            grid=(4,),
            in_specs=[
                pl.BlockSpec((depth, rows), lambda r, z, c: (0, 0)),
                pl.BlockSpec((depth, cols), lambda r, z, c: (0, target(z, r) * 2 + c[0])),
                pl.BlockSpec((1, rows, cols), lambda r, z, c: (r, 0, 0)),
            ],
            out_specs=(
                at(lambda r: jnp.where(r == 0, 1, 0)),
                at(lambda r: jnp.where(r == 3, 0, 1)),
                at(lambda r: jnp.where(r == 0, 1, 0)),
                at(lambda r: jnp.where(r >= 2, 0, 1)),
            ),
        ),
        compiler_params=params(LIM),
        cost_estimate=pl.CostEstimate(flops=4 * 2 * rows * cols * depth, bytes_accessed=7 * 2**20, transcendentals=0),
        name="project_own",
    )(z, c, out_grad, out_weight, peer)


def onward_kernel(keep, recv, own, out):
    for i, ref in enumerate((own, out)):
        ref[...] = (keep[i].astype(jnp.float32) + recv[i].astype(jnp.float32)).astype(jnp.bfloat16)


def onward(keep, recv):
    out = jax.ShapeDtypeStruct(keep.shape[1:], jnp.bfloat16)
    return pl.pallas_call(
        onward_kernel,
        out_shape=(out, out),
        in_specs=specs(VMEM, 2),
        out_specs=tuple(specs(VMEM, 2)),
        compiler_params=params(4),
        name="onward",
    )(keep, recv)


def attend_head(a, meta, q, k, v, gathered, parts, dq, dk, dv, ret, scratch):
    kc, vc, kt, qc, gc, gsum, dkc, dvc, ex, fx, dp = scratch
    gsum[...] = (parts[0][...].astype(jnp.float32) + parts[1][...].astype(jnp.float32)).astype(jnp.bfloat16)
    cols = slice(a * HD, (a + 1) * HD)
    for p in range(16):
        dev, src = place(meta[PLIST + p])
        kc[p * BLK : (p + 1) * BLK, :] = gathered[dev, src, :HD]
        vc[p * BLK : (p + 1) * BLK, :] = gathered[dev, src, HD:]

    lane = lax.broadcasted_iota(jnp.int32, (8, ROWS), 1)
    plim = jnp.zeros((8, ROWS), jnp.int32)
    llim = jnp.zeros((8, ROWS), jnp.int32)
    for j in range(BLK_DEV):
        src = rows_at(meta[ORDER + j])
        kc[PKEYS + j * BLK : PKEYS + (j + 1) * BLK, :] = k[src, cols]
        vc[PKEYS + j * BLK : PKEYS + (j + 1) * BLK, :] = v[src, cols]
        for h in range(2):
            to = slice(h * ROWS + j * BLK, h * ROWS + (j + 1) * BLK)
            qc[to, :] = q[src, (2 * a + h) * HD : (2 * a + h + 1) * HD]
            gc[to, :] = gsum[src, h * HD : (h + 1) * HD]
        here = (lane >= j * BLK) & (lane < (j + 1) * BLK)
        resp = meta[RESP + j]
        step = lane - (j * BLK - 1)
        plim = jnp.where(here, meta[BASE + j] + step * (1 - resp), plim)
        llim = jnp.where(here, (j * BLK + step) * resp, llim)
    kt[...] = kc[...].T
    sub = lax.broadcasted_iota(jnp.int32, (CHUNK, CHUNK), 0)

    for h in range(2):
        for half in range(ROWS // CHUNK):
            rows = slice(h * ROWS + half * CHUNK, h * ROWS + (half + 1) * CHUNK)
            qb = qc[rows, :]
            gb = gc[rows, :]
            lanes = slice(half * CHUNK, (half + 1) * CHUNK)
            pl_row = plim[:1, lanes]
            ll_row = llim[:1, lanes]
            chunks = PKEYS // CHUNK + half + 1
            total = jnp.zeros((1, CHUNK), jnp.float32)
            weighted = jnp.zeros((1, CHUNK), jnp.float32)
            for c in range(chunks):
                cut = slice(c * CHUNK, (c + 1) * CHUNK)
                raw = lax.dot_general(kc[cut, :], qb, NT, preferred_element_type=jnp.float32)
                dprob = lax.dot_general(vc[cut, :], gb, NT, preferred_element_type=jnp.float32)
                tanh_val = jnp.tanh(raw * (SCALE / SOFTCAP))
                if c * CHUNK < PKEYS:
                    seen = sub < pl_row - c * CHUNK
                else:
                    seen = sub < ll_row - (c * CHUNK - PKEYS)
                expo = jnp.where(seen, jnp.exp(SOFTCAP * tanh_val), 0.0)
                total = total + jnp.sum(expo, axis=0, keepdims=True)
                weighted = weighted + jnp.sum(expo * dprob, axis=0, keepdims=True)
                ex[cut, :] = expo
                fx[cut, :] = expo * (1.0 - tanh_val * tanh_val)
                dp[cut, :] = dprob
            inv = 1.0 / total
            delta = weighted * inv
            scaled = inv * SCALE
            dq_t = jnp.zeros((HD, CHUNK), jnp.float32)
            for c in range(chunks):
                cut = slice(c * CHUNK, (c + 1) * CHUNK)
                prob16 = (ex[cut, :] * inv).astype(jnp.bfloat16)
                dscore16 = (fx[cut, :] * ((dp[cut, :] - delta) * scaled)).astype(jnp.bfloat16)
                dv_part = jnp.dot(prob16, gb, preferred_element_type=jnp.float32)
                dk_part = jnp.dot(dscore16, qb, preferred_element_type=jnp.float32)
                dq_t = dq_t + jnp.dot(kt[:, cut], dscore16, preferred_element_type=jnp.float32)
                if h == 0 and (half == 0 or c == PKEYS // CHUNK + 1):
                    dvc[cut, :] = dv_part
                    dkc[cut, :] = dk_part
                else:
                    dvc[cut, :] += dv_part
                    dkc[cut, :] += dk_part
            dq_rows = dq_t.T.astype(jnp.bfloat16)
            for j in range(CHUNK // BLK):
                dst = rows_at(meta[ORDER + half * (CHUNK // BLK) + j])
                dq[dst, h * HD : (h + 1) * HD] = dq_rows[j * BLK : (j + 1) * BLK, :]

    ret[...] = jnp.zeros(ret.shape, ret.dtype)
    for p in range(16):
        dev, dst = place(meta[PLIST + p])
        src = slice(p * BLK, (p + 1) * BLK)
        ret[dev, dst, :HD] = dkc[src, :].astype(jnp.bfloat16)
        ret[dev, dst, HD:] = dvc[src, :].astype(jnp.bfloat16)
    for j in range(BLK_DEV):
        dst = rows_at(meta[ORDER + j])
        src = slice(PKEYS + j * BLK, PKEYS + (j + 1) * BLK)
        dk[dst, cols] = dkc[src, :].astype(jnp.bfloat16)
        dv[dst, cols] = dvc[src, :].astype(jnp.bfloat16)


def attend_kernel(
    meta, q, k, v, gathered, own_a, last_a, own_b, last_b,
    dq, dk, dv, ret,
    qs, ks, vs, gs, ps, dqs, dks, dvs, rets, sem_in, sem_out, *scratch,
):
    loads = [
        (own_a, ps.at[0, 0]), (last_a, ps.at[0, 1]), (gathered.at[:, 0], gs.at[0]), (k, ks), (v, vs), (q, qs),
        (own_b, ps.at[1, 0]), (last_b, ps.at[1, 1]), (gathered.at[:, 1], gs.at[1]),
    ]
    loads = [pltpu.make_async_copy(src, dst, sem_in.at[i]) for i, (src, dst) in enumerate(loads)]
    for copy in loads:
        copy.start()
    stores = [
        (rets.at[0], ret.at[:, 0]), (dqs.at[0], dq.at[:, pl.ds(0, 2 * HD)]),
        (rets.at[1], ret.at[:, 1]), (dqs.at[1], dq.at[:, pl.ds(2 * HD, 2 * HD)]), (dks, dk), (dvs, dv),
    ]
    stores = [pltpu.make_async_copy(src, dst, sem_out.at[i]) for i, (src, dst) in enumerate(stores)]
    for a in range(2):
        for copy in loads[6 * a : 6 + 3 * a]:
            copy.wait()
        parts = [ps.at[a, i] for i in range(2)]
        attend_head(a, meta, qs, ks, vs, gs.at[a], parts, dqs.at[a], dks, dvs, rets.at[a], scratch)
        for copy in stores[2 * a : 2 + 4 * a]:
            copy.start()
    for copy in stores:
        copy.wait()


def attend(meta, queries, keys, values, gathered, parts):
    return pl.pallas_call(
        attend_kernel,
        out_shape=(
            jax.ShapeDtypeStruct(queries.shape, jnp.bfloat16),
            jax.ShapeDtypeStruct(keys.shape, jnp.bfloat16),
            jax.ShapeDtypeStruct(values.shape, jnp.bfloat16),
            jax.ShapeDtypeStruct(gathered.shape, jnp.bfloat16),
        ),
        in_specs=specs(SMEM, 1) + specs(pl.ANY, 8),
        out_specs=tuple(specs(pl.ANY, 4)),
        scratch_shapes=[
            pltpu.VMEM(queries.shape, jnp.bfloat16),
            pltpu.VMEM(keys.shape, jnp.bfloat16),
            pltpu.VMEM(values.shape, jnp.bfloat16),
            pltpu.VMEM((2, DEVS, PCAP * BLK, 2 * HD), jnp.bfloat16),
            pltpu.VMEM((2, 2, ROWS, 2 * HD), jnp.bfloat16),
            pltpu.VMEM((2, ROWS, 2 * HD), jnp.bfloat16),
            pltpu.VMEM(keys.shape, jnp.bfloat16),
            pltpu.VMEM(values.shape, jnp.bfloat16),
            pltpu.VMEM((2, DEVS, PCAP * BLK, 2 * HD), jnp.bfloat16),
            pltpu.SemaphoreType.DMA((9,)),
            pltpu.SemaphoreType.DMA((6,)),
            pltpu.VMEM((KEYS, HD), jnp.bfloat16),
            pltpu.VMEM((KEYS, HD), jnp.bfloat16),
            pltpu.VMEM((HD, KEYS), jnp.bfloat16),
            pltpu.VMEM((2 * ROWS, HD), jnp.bfloat16),
            pltpu.VMEM((2 * ROWS, HD), jnp.bfloat16),
            pltpu.VMEM((ROWS, 2 * HD), jnp.bfloat16),
            pltpu.VMEM((KEYS, HD), jnp.float32),
            pltpu.VMEM((KEYS, HD), jnp.float32),
            pltpu.VMEM((KEYS, CHUNK), jnp.float32),
            pltpu.VMEM((KEYS, CHUNK), jnp.float32),
            pltpu.VMEM((KEYS, CHUNK), jnp.float32),
        ],
        compiler_params=params(LIM),
        cost_estimate=pl.CostEstimate(flops=4 * 10**9, bytes_accessed=8 * 2**20, transcendentals=6 * 10**6),
        name="attend",
    )(meta, queries, keys, values, gathered, *parts)


def finish_kernel(meta, own_k, own_v, ret, dk, dv):
    for i, (own, out) in enumerate(((own_k, dk), (own_v, dv))):
        out[...] = own[...]
        for r in range(PCAP):

            @pl.when(meta[COUNT] > r)
            def _(r=r, i=i, out=out):
                rows = slice(r * BLK, (r + 1) * BLK)
                for a in range(2):
                    total = ret[0, a, rows, i * HD : (i + 1) * HD].astype(jnp.float32)
                    for d in range(1, DEVS):
                        total = total + ret[d, a, rows, i * HD : (i + 1) * HD].astype(jnp.float32)
                    at = rows_at(meta[ORDER + BLK_DEV - 1 - r])
                    out[at, a * HD : (a + 1) * HD] = total.astype(jnp.bfloat16)


def finish(meta, own_k, own_v, ret):
    out = jax.ShapeDtypeStruct(own_k.shape, jnp.bfloat16)
    return pl.pallas_call(
        finish_kernel,
        out_shape=(out, out),
        in_specs=specs(SMEM, 1) + specs(VMEM, 3),
        out_specs=tuple(specs(VMEM, 2)),
        compiler_params=params(8),
        name="finish",
    )(meta, own_k, own_v, ret)


def scalar(axis):
    return lax.axis_index(axis).astype(jnp.int32).reshape(1)


def shards(out_grad, out_weight, query_states, key_states, value_states, slot_seq, slot_pos, fork_depth):
    here, z, c = scalar("seq"), scalar("mp"), scalar("section")
    pair_a = [(i, i ^ 1) for i in range(4)]
    pair_b = [(i, 3 - i) for i in range(4)]
    out_grad, out_weight = out_grad.T, out_weight.T

    slots = (slot_seq, slot_pos, fork_depth)
    peer, meta, prompt = project_peer(z, c, here, out_grad, out_weight, *slots, key_states, value_states)
    peer = lax.ppermute(peer, "section", [(0, 1), (1, 0)])
    gathered = lax.all_to_all(prompt, "seq", 0, 0, tiled=True)
    send_a, keep_a, send_b, keep_b = project_own(z, c, out_grad, out_weight, peer)
    recv_a = lax.ppermute(send_a, "mp", pair_a)
    recv_b = lax.ppermute(send_b, "mp", pair_b)
    own_a, next_a = onward(keep_a, recv_a)
    last_a = lax.ppermute(next_a, "mp", pair_b)
    own_b, next_b = onward(keep_b, recv_b)
    last_b = lax.ppermute(next_b, "mp", pair_a)
    parts = (own_a, last_a, own_b, last_b)
    dq, own_k, own_v, ret = attend(meta, query_states, key_states, value_states, gathered, parts)
    ret = lax.all_to_all(ret, "seq", 0, 0, tiled=True)
    dk, dv = finish(meta, own_k, own_v, ret)
    return dq, dk, dv


def solution(mesh):
    wide = P("seq", ("mp", "section"))
    return jax.shard_map(
        shards,
        mesh=mesh,
        in_specs=(wide, P(None, ("mp", "section")), wide, wide, wide, P(), P(), P()),
        out_specs=(wide, wide, wide),
        check_vma=False,
    )
```

time: 114 us -> 102 us (0.89)
  local copies, waits for them, and re-layouts: 16.1 us -> 3.75 us
  waiting for transfers between devices: 22.3 us -> 17.3 us
  starting transfers between devices: 13.1 us -> 15.6 us
  Pallas kernels: 28.2 us -> 30.6 us
    unnamed x28 -> x20, local copies, waits for them, and re-layouts: 16.1 us -> 3.75 us
    ppermute x1, waiting for transfers between devices: 12.3 us -> 0.01 us  [shards(): recv_b = lax.ppermute(send_b, 'mp', pair_b)]
    ppermute x1, waiting for transfers between devices: 1.3 us -> 9.97 us  [shards(): recv_a = lax.ppermute(send_a, 'mp', pair_a)]
    pallas_call x1, Pallas kernels: 3.32 us -> 5.98 us  [project_own(): pl.pallas_call(project_own_kernel, out_shape=(part, part, part, part), gr...]
    ppermute x1, starting transfers between devices: 1.75 us -> 3.94 us  [shards(): last_a = lax.ppermute(next_a, 'mp', pair_b)]
    all_to_all x1, waiting for transfers between devices: 8.68 us -> 6.73 us  [shards(): gathered = lax.all_to_all(prompt, 'seq', 0, 0, tiled=True)]
    ppermute x1, starting transfers between devices: 0.01 us -> 1.92 us  [shards(): recv_a = lax.ppermute(send_a, 'mp', pair_a)]
    ppermute x1, starting transfers between devices: 4.12 us -> 2.52 us  [shards(): recv_b = lax.ppermute(send_b, 'mp', pair_b)]
  transfers between devices with their start and end apart: 6 -> 6, of which waited for: 3 -> 3; matrix products, arithmetic and copies ran while one was open for 0% -> 0% of each run, Pallas kernels for 5% -> 6%
where the time goes in v2:
time: 102 us; the launch traced here: 101 us
  blocking collectives  33.1 us (32%)
  Pallas kernels  30.6 us (30%)
  waiting for transfers between devices  17.3 us (17%)
  starting transfers between devices  15.6 us (15%)
  local copies, waits for them, and re-layouts  3.75 us (4%)
    all_to_all x1, blocking collectives, shards(): ret = lax.all_to_all(ret, 'seq', 0, 0, tiled=True)  33.1 us
    pallas_call x1, Pallas kernels, attend(): pl.pallas_call(attend_kernel, out_shape=(jax.ShapeDtypeStruct(queries.sha...  16.3 us
    ppermute x1, waiting for transfers between devices, shards(): recv_a = lax.ppermute(send_a, 'mp', pair_a)  9.97 us
    all_to_all x1, starting transfers between devices, shards(): gathered = lax.all_to_all(prompt, 'seq', 0, 0, tiled=True)  7.12 us
    all_to_all x1, waiting for transfers between devices, shards(): gathered = lax.all_to_all(prompt, 'seq', 0, 0, tiled=True)  6.73 us
    pallas_call x1, Pallas kernels, project_peer(): pl.pallas_call(project_peer_kernel, out_shape=(jax.ShapeDtypeStruct((4, r...  6.43 us
    pallas_call x1, Pallas kernels, project_own(): pl.pallas_call(project_own_kernel, out_shape=(part, part, part, part), gr...  5.98 us
    ppermute x1, starting transfers between devices, shards(): last_a = lax.ppermute(next_a, 'mp', pair_b)  3.94 us
  transfers between devices with their start and end apart: 6, of which 3 were waited for; matrix products, arithmetic and copies ran while one was open for 0% of the time, Pallas kernels for 6%

profile of v2, /device:TPU:0, one launch (start us, length us, event | category | flops | bytes accessed | tf_op | source)
XLA Modules:
  0.0 101.1 jit_solution(18014576658254736060)
XLA Ops:
  0.6 6.4 %project_peer.1 = (bf16[4,512,512]{2,1,0:T(8,128)(2,1)}, s32[48]{0:T(128)}, bf16[16,2,128,256]{3,2,1,0:T(8,128)(2,1)}) custom-call(s32[1]{0:T(128)} %bitcast.z, s32[1]{0:T(128)} %bitcast.1.c, s32[1]{0:T(128)} %bitcast.2.here, bf16[576,512]{1,0:T(8,128)(2,1)} %bitcast.7, bf16[576,4096]{1,0:T(8,128)(2,1)} %bitcast.5, s32[128]{0:T(128)} %seq.1, s32[128]{0:T(128)} %pos.1, ...), custom_call_target="tpu_custom_call" | custom-call | flops 1207959552 | bytes 5242880 | tf_op jit(solution)/shard_map/project_peer/pallas_call | solution.py:117
  7.1 0.1 collective-permute-start
  7.2 7.1 %all-to-all-start = ((bf16[16,2,128,256]{3,2,1,0:T(8,128)(2,1)}), bf16[16,2,128,256]{3,2,1,0:T(8,128)(2,1)S(1)}, u32[]{:S(2)}, u32[]{:S(2)}) async-start(bf16[16,2,128,256]{3,2,1,0:T(8,128)(2,1)} %get-tuple-element.21), calls=%async_computation | async-start | bytes 4194304 | tf_op jit(solution)/shard_map/all_to_all | solution.py:419
  14.3 0.0 collective-permute-done.peer
  14.3 6.0 %project_own.1 = (bf16[2,512,256]{2,1,0:T(8,128)(2,1)}, bf16[2,512,256]{2,1,0:T(8,128)(2,1)}, bf16[2,512,256]{2,1,0:T(8,128)(2,1)}, bf16[2,512,256]{2,1,0:T(8,128)(2,1)}) custom-call(s32[1]{0:T(128)} %bitcast.z, s32[1]{0:T(128)} %bitcast.1.c, bf16[576,512]{1,0:T(8,128)(2,1)} %bitcast.8, bf16[576,4096]{1,0:T(8,128)(2,1)} %bitcast.6, ...), custom_call_target="tpu_custom_call" | custom-call | flops 1207959552 | bytes 7340032 | tf_op jit(solution)/shard_map/project_own/pallas_call | solution.py:179
  20.3 1.9 %collective-permute-start.1 = (bf16[2,512,256]{2,1,0:T(8,128)(2,1)}, bf16[2,512,256]{2,1,0:T(8,128)(2,1)S(1)}, u32[]{:S(2)}, u32[]{:S(2)}) collective-permute-start(bf16[2,512,256]{2,1,0:T(8,128)(2,1)} %get-tuple-element.24), channel_id=1, source_target_pairs={{0,2},{2,0},{4,6},{6,4},{1,3},{3,1},{5,7},{7,5},{8,10},{10,8},{12,... | collective-permute-start | bytes 1572872 | tf_op jit(solution)/shard_map/ppermute | solution.py:421
  22.2 2.5 %collective-permute-start.3 = (bf16[2,512,256]{2,1,0:T(8,128)(2,1)}, bf16[2,512,256]{2,1,0:T(8,128)(2,1)S(1)}, u32[]{:S(2)}, u32[]{:S(2)}) collective-permute-start(bf16[2,512,256]{2,1,0:T(8,128)(2,1)} %get-tuple-element.28), channel_id=1, source_target_pairs={{0,6},{2,4},{4,2},{6,0},{1,7},{3,5},{5,3},{7,1},{8,14},{10,12},{12... | collective-permute-start | bytes 1572872 | tf_op jit(solution)/shard_map/ppermute | solution.py:422
  24.7 10.0 %collective-permute-done.1.recv = bf16[2,512,256]{2,1,0:T(8,128)(2,1)S(1)} collective-permute-done((bf16[2,512,256]{2,1,0:T(8,128)(2,1)}, bf16[2,512,256]{2,1,0:T(8,128)(2,1)S(1)}, u32[]{:S(2)}, u32[]{:S(2)}) %collective-permute-start.1) | collective-permute-done | bytes 524320 | tf_op jit(solution)/shard_map/ppermute | solution.py:421
  34.7 1.0 %copy-done.1 = bf16[2,512,256]{2,1,0:T(8,128)(2,1)S(1)} copy-done((bf16[2,512,256]{2,1,0:T(8,128)(2,1)S(1)}, bf16[2,512,256]{2,1,0:T(8,128)(2,1)}, u32[]{:S(2)}) %copy-start.1) | copy-done | bytes 524312
  35.8 0.1 onward.2
  35.9 0.0 copy-start.5
  35.9 3.9 %collective-permute-start.2 = (bf16[512,256]{1,0:T(8,128)(2,1)S(1)}, bf16[512,256]{1,0:T(8,128)(2,1)S(1)}, u32[]{:S(2)}, u32[]{:S(2)}) collective-permute-start(bf16[512,256]{1,0:T(8,128)(2,1)S(1)} %get-tuple-element.26), channel_id=1, source_target_pairs={{0,6},{2,4},{4,2},{6,0},{1,7},{3,5},{5,3},{7,1},{8,14},{10,12},{12... | collective-permute-start | bytes 786440 | tf_op jit(solution)/shard_map/ppermute | solution.py:424
  39.8 0.0 collective-permute-done.3.recv
  39.8 1.0 %copy-done = bf16[2,512,256]{2,1,0:T(8,128)(2,1)S(1)} copy-done((bf16[2,512,256]{2,1,0:T(8,128)(2,1)S(1)}, bf16[2,512,256]{2,1,0:T(8,128)(2,1)}, u32[]{:S(2)}) %copy-start) | copy-done | bytes 524312
  40.9 0.1 onward.3
  41.0 0.0 copy-done.5
  41.0 0.0 copy-start.6
  41.0 0.7 copy-done.6
  41.7 0.0 collective-permute-start.4
  41.7 6.7 %all-to-all-done.gathered = bf16[16,2,128,256]{3,2,1,0:T(8,128)(2,1)S(1)} async-done(((bf16[16,2,128,256]{3,2,1,0:T(8,128)(2,1)}), bf16[16,2,128,256]{3,2,1,0:T(8,128)(2,1)S(1)}, u32[]{:S(2)}, u32[]{:S(2)}) %all-to-all-start) | async-done | bytes 2097184 | tf_op jit(solution)/shard_map/all_to_all | solution.py:419
  48.5 0.0 collective-permute-done.2.last_a
  48.5 0.6 collective-permute-done.4.last_b
  49.0 0.8 copy-done.7
  49.8 0.1 copy-done.8
  49.9 0.1 copy-done.9
  50.0 16.3 %attend.1 = (bf16[512,512]{1,0:T(8,128)(2,1)}, bf16[512,256]{1,0:T(8,128)(2,1)}, bf16[512,256]{1,0:T(8,128)(2,1)}, bf16[16,2,128,256]{3,2,1,0:T(8,128)(2,1)}) custom-call(s32[48]{0:T(128)} %get-tuple-element.20.meta, bf16[512,512]{1,0:T(8,128)(2,1)} %q.1, bf16[512,256]{1,0:T(8,128)(2,1)} %k.1, bf16[512,256]{1,0:T(8,128)(2,1)} %v.1, ...), custom_call_target="tpu_custom_call" | custom-call | flops 4000000000 | bytes 8388608 | tf_op jit(solution)/shard_map/attend/pallas_call | solution.py:338
  66.3 0.0 copy-start.2
  66.3 0.0 copy-start.3
  66.3 0.0 copy-start.4
  66.3 33.1 %all_to_all.10.ret = bf16[16,2,128,256]{3,2,1,0:T(8,128)(2,1)S(1)} all-to-all(bf16[16,2,128,256]{3,2,1,0:T(8,128)(2,1)} %get-tuple-element.34), channel_id=1, replica_groups=mesh['seq'=16,'mp'=4,'section'=2] {'seq'}, dimensions={0} | all-to-all | bytes 4194304 | tf_op jit(solution)/shard_map/all_to_all | solution.py:429
  99.4 0.0 copy-done.2
  99.4 1.7 %finish.1 = (bf16[512,256]{1,0:T(8,128)(2,1)}, bf16[512,256]{1,0:T(8,128)(2,1)}) custom-call(s32[48]{0:T(128)S(1)} %copy-done.4, bf16[512,256]{1,0:T(8,128)(2,1)S(1)} %copy-done.2, bf16[512,256]{1,0:T(8,128)(2,1)S(1)} %copy-done.3, bf16[16,2,128,256]{3,2,1,0:T(8,128)(2,1)S(1)} %all_to_all.10.ret), custom_call_target="tpu_custom_call" | custom-call | tf_op jit(solution)/shard_map/finish/pallas_call | solution.py:396
  (7 shorter events, 0.0 us)
Async XLA Ops:
  7.1 7.2 %collective-permute-start = (bf16[4,512,512]{2,1,0:T(8,128)(2,1)}, bf16[4,512,512]{2,1,0:T(8,128)(2,1)}, u32[]{:S(2)}, u32[]{:S(2)}) collective-permute-start(bf16[4,512,512]{2,1,0:T(8,128)(2,1)} %get-tuple-element.22), channel_id=1, source_target_pairs={{0,1},{1,0},{2,3},{3,2},{4,5},{5,4},{6,7},{7,6},{8,9},{9,8},{10,11... | collective-permute-start | bytes 6291464 | tf_op jit(solution)/shard_map/ppermute | solution.py:418
  7.2 41.3 %all-to-all-start = ((bf16[16,2,128,256]{3,2,1,0:T(8,128)(2,1)}), bf16[16,2,128,256]{3,2,1,0:T(8,128)(2,1)S(1)}, u32[]{:S(2)}, u32[]{:S(2)}) async-start(bf16[16,2,128,256]{3,2,1,0:T(8,128)(2,1)} %get-tuple-element.21), calls=%async_computation | async-start | bytes 4194304 | tf_op jit(solution)/shard_map/all_to_all | solution.py:419
  20.3 14.4 %collective-permute-start.1 = (bf16[2,512,256]{2,1,0:T(8,128)(2,1)}, bf16[2,512,256]{2,1,0:T(8,128)(2,1)S(1)}, u32[]{:S(2)}, u32[]{:S(2)}) collective-permute-start(bf16[2,512,256]{2,1,0:T(8,128)(2,1)} %get-tuple-element.24), channel_id=1, source_target_pairs={{0,2},{2,0},{4,6},{6,4},{1,3},{3,1},{5,7},{7,5},{8,10},{10,8},{12,... | collective-permute-start | bytes 1572872 | tf_op jit(solution)/shard_map/ppermute | solution.py:421
  22.2 17.6 %collective-permute-start.3 = (bf16[2,512,256]{2,1,0:T(8,128)(2,1)}, bf16[2,512,256]{2,1,0:T(8,128)(2,1)S(1)}, u32[]{:S(2)}, u32[]{:S(2)}) collective-permute-start(bf16[2,512,256]{2,1,0:T(8,128)(2,1)} %get-tuple-element.28), channel_id=1, source_target_pairs={{0,6},{2,4},{4,2},{6,0},{1,7},{3,5},{5,3},{7,1},{8,14},{10,12},{12... | collective-permute-start | bytes 1572872 | tf_op jit(solution)/shard_map/ppermute | solution.py:422
  34.7 1.0 %copy-start.1 = (bf16[2,512,256]{2,1,0:T(8,128)(2,1)S(1)}, bf16[2,512,256]{2,1,0:T(8,128)(2,1)}, u32[]{:S(2)}) copy-start(bf16[2,512,256]{2,1,0:T(8,128)(2,1)} %get-tuple-element.23.keep) | copy-start | bytes 1572868
  35.9 5.1 %copy-start.5 = (bf16[512,256]{1,0:T(8,128)(2,1)}, bf16[512,256]{1,0:T(8,128)(2,1)S(1)}, u32[]{:S(2)}) copy-start(bf16[512,256]{1,0:T(8,128)(2,1)S(1)} %get-tuple-element.25.own_a) | copy-start | bytes 786436
  35.9 12.6 %collective-permute-start.2 = (bf16[512,256]{1,0:T(8,128)(2,1)S(1)}, bf16[512,256]{1,0:T(8,128)(2,1)S(1)}, u32[]{:S(2)}, u32[]{:S(2)}) collective-permute-start(bf16[512,256]{1,0:T(8,128)(2,1)S(1)} %get-tuple-element.26), channel_id=1, source_target_pairs={{0,6},{2,4},{4,2},{6,0},{1,7},{3,5},{5,3},{7,1},{8,14},{10,12},{12... | collective-permute-start | bytes 786440 | tf_op jit(solution)/shard_map/ppermute | solution.py:424
  39.8 1.0 %copy-start = (bf16[2,512,256]{2,1,0:T(8,128)(2,1)S(1)}, bf16[2,512,256]{2,1,0:T(8,128)(2,1)}, u32[]{:S(2)}) copy-start(bf16[2,512,256]{2,1,0:T(8,128)(2,1)} %get-tuple-element.27.keep) | copy-start | bytes 1572868
  41.0 0.7 copy-start.6
  41.7 7.3 %collective-permute-start.4 = (bf16[512,256]{1,0:T(8,128)(2,1)S(1)}, bf16[512,256]{1,0:T(8,128)(2,1)S(1)}, u32[]{:S(2)}, u32[]{:S(2)}) collective-permute-start(bf16[512,256]{1,0:T(8,128)(2,1)S(1)} %get-tuple-element.30), channel_id=1, source_target_pairs={{0,2},{2,0},{4,6},{6,4},{1,3},{3,1},{5,7},{7,5},{8,10},{10,8},{12,... | collective-permute-start | bytes 786440 | tf_op jit(solution)/shard_map/ppermute | solution.py:426
  48.5 1.3 %copy-start.7 = (bf16[16,2,128,256]{3,2,1,0:T(8,128)(2,1)}, bf16[16,2,128,256]{3,2,1,0:T(8,128)(2,1)S(1)}, u32[]{:S(2)}) copy-start(bf16[16,2,128,256]{3,2,1,0:T(8,128)(2,1)S(1)} %all-to-all-done.gathered) | copy-start | bytes 6291460
  48.5 1.4 %copy-start.8 = (bf16[512,256]{1,0:T(8,128)(2,1)}, bf16[512,256]{1,0:T(8,128)(2,1)S(1)}, u32[]{:S(2)}) copy-start(bf16[512,256]{1,0:T(8,128)(2,1)S(1)} %collective-permute-done.2.last_a) | copy-start | bytes 786436
  49.0 0.9 copy-start.9
  66.3 33.2 %copy-start.2 = (bf16[512,256]{1,0:T(8,128)(2,1)S(1)}, bf16[512,256]{1,0:T(8,128)(2,1)}, u32[]{:S(2)}) copy-start(bf16[512,256]{1,0:T(8,128)(2,1)} %get-tuple-element.32.own_k) | copy-start | bytes 786436
  66.3 33.2 %copy-start.3 = (bf16[512,256]{1,0:T(8,128)(2,1)S(1)}, bf16[512,256]{1,0:T(8,128)(2,1)}, u32[]{:S(2)}) copy-start(bf16[512,256]{1,0:T(8,128)(2,1)} %get-tuple-element.33.own_v) | copy-start | bytes 786436
  66.3 33.2 %copy-start.4 = (s32[48]{0:T(128)S(1)}, s32[48]{0:T(128)}, u32[]{:S(2)}) copy-start(s32[48]{0:T(128)} %get-tuple-element.20.meta) | copy-start | bytes 580

commit v3 on v2

--- a/solution.py
+++ b/solution.py
@@ -17,18 +17,22 @@
 
 SCALE = 144.0 ** (-0.5)
 SOFTCAP = 50.0
+LOG2E = 1.4426950408889634
 
 PLIST = 0
 ORDER = 16
 BASE = 24
 RESP = 32
 COUNT = 40
+SPARE = 41
 META = 48
 
 LIM = 60
+OWNLIM = 60
 
 SMEM = pltpu.MemorySpace.SMEM
 VMEM = pltpu.MemorySpace.VMEM
+HBM = pltpu.MemorySpace.HBM
 NT = (((1,), (1,)), ((), ()))
 TN = (((0,), (0,)), ((), ()))
 
@@ -52,20 +56,15 @@
 def make_layout(here, seq, pos, depth, keys, values, meta, block):
     me = here[0]
 
-    def device(dev, carry):
+    for dev in range(DEVS):
         count = jnp.int32(0)
         for b in range(BLK_DEV):
             slot = dev * BLK_DEV + b
             prompt = seq[slot] == 0
-
-            @pl.when(prompt)
-            def _(count=count, slot=slot):
-                meta[PLIST + pos[slot]] = dev * PCAP + jnp.minimum(count, PCAP - 1)
-
+            at = jnp.where(prompt, PLIST + pos[slot], SPARE)
+            meta[at] = dev * PCAP + jnp.minimum(count, PCAP - 1)
             count = count + prompt.astype(jnp.int32)
-        return carry
-
-    lax.fori_loop(0, DEVS, device, 0)
+
     count = jnp.int32(0)
     block[...] = jnp.zeros(block.shape, block.dtype)
     for b in range(BLK_DEV):
@@ -96,13 +95,19 @@
     r = pl.program_id(0)
     copies = [pltpu.make_async_copy(block, prompt.at[d], sems.at[d]) for d in range(DEVS)]
 
+    def product():
+        out[0] = lax.dot_general(grad[...], weight[...], TN, preferred_element_type=jnp.float32).astype(jnp.bfloat16)
+
     @pl.when(r == 0)
     def _():
         make_layout(here, seq, pos, depth, keys, values, meta, block)
         for copy in copies:
             copy.start()
-
-    out[0] = lax.dot_general(grad[...], weight[...], TN, preferred_element_type=jnp.float32).astype(jnp.bfloat16)
+        product()
+
+    @pl.when(r > 0)
+    def _():
+        product()
 
     @pl.when(r == 3)
     def _():
@@ -194,31 +199,30 @@
                 at(lambda r: jnp.where(r >= 2, 0, 1)),
             ),
         ),
-        compiler_params=params(LIM),
+        compiler_params=params(OWNLIM),
         cost_estimate=pl.CostEstimate(flops=4 * 2 * rows * cols * depth, bytes_accessed=7 * 2**20, transcendentals=0),
         name="project_own",
     )(z, c, out_grad, out_weight, peer)
 
 
-def onward_kernel(keep, recv, own, out):
-    for i, ref in enumerate((own, out)):
-        ref[...] = (keep[i].astype(jnp.float32) + recv[i].astype(jnp.float32)).astype(jnp.bfloat16)
-
-
-def onward(keep, recv):
-    out = jax.ShapeDtypeStruct(keep.shape[1:], jnp.bfloat16)
-    return pl.pallas_call(
-        onward_kernel,
-        out_shape=(out, out),
-        in_specs=specs(VMEM, 2),
-        out_specs=tuple(specs(VMEM, 2)),
-        compiler_params=params(4),
-        name="onward",
-    )(keep, recv)
+def visible(meta, seen):
+    lane = lax.broadcasted_iota(jnp.int32, (8, ROWS), 1)
+    prompt = jnp.zeros((8, ROWS), jnp.int32)
+    own = jnp.zeros((8, ROWS), jnp.int32)
+    for j in range(BLK_DEV):
+        here = (lane >= j * BLK) & (lane < (j + 1) * BLK)
+        resp = meta[RESP + j]
+        step = lane - (j * BLK - 1)
+        prompt = jnp.where(here, meta[BASE + j] + step * (1 - resp), prompt)
+        own = jnp.where(here, (j * BLK + step) * resp, own)
+    row = lax.broadcasted_iota(jnp.int32, (8, ROWS), 0)
+    for start, limit, size in ((0, prompt - row, PKEYS), (PKEYS, own - row, ROWS)):
+        for r in range(0, size, 8):
+            seen[start + r : start + r + 8, :] = jnp.where(limit > r, 1.0, 0.0)
 
 
 def attend_head(a, meta, q, k, v, gathered, parts, dq, dk, dv, ret, scratch):
-    kc, vc, kt, qc, gc, gsum, dkc, dvc, ex, fx, dp = scratch
+    kc, vc, kt, qc, gc, gsum, dkc, dvc, ex, fx, dp, seen = scratch
     gsum[...] = (parts[0][...].astype(jnp.float32) + parts[1][...].astype(jnp.float32)).astype(jnp.bfloat16)
     cols = slice(a * HD, (a + 1) * HD)
     for p in range(16):
@@ -226,9 +230,6 @@
         kc[p * BLK : (p + 1) * BLK, :] = gathered[dev, src, :HD]
         vc[p * BLK : (p + 1) * BLK, :] = gathered[dev, src, HD:]
 
-    lane = lax.broadcasted_iota(jnp.int32, (8, ROWS), 1)
-    plim = jnp.zeros((8, ROWS), jnp.int32)
-    llim = jnp.zeros((8, ROWS), jnp.int32)
     for j in range(BLK_DEV):
         src = rows_at(meta[ORDER + j])
         kc[PKEYS + j * BLK : PKEYS + (j + 1) * BLK, :] = k[src, cols]
@@ -237,57 +238,58 @@
             to = slice(h * ROWS + j * BLK, h * ROWS + (j + 1) * BLK)
             qc[to, :] = q[src, (2 * a + h) * HD : (2 * a + h + 1) * HD]
             gc[to, :] = gsum[src, h * HD : (h + 1) * HD]
-        here = (lane >= j * BLK) & (lane < (j + 1) * BLK)
-        resp = meta[RESP + j]
-        step = lane - (j * BLK - 1)
-        plim = jnp.where(here, meta[BASE + j] + step * (1 - resp), plim)
-        llim = jnp.where(here, (j * BLK + step) * resp, llim)
     kt[...] = kc[...].T
-    sub = lax.broadcasted_iota(jnp.int32, (CHUNK, CHUNK), 0)
-
-    for h in range(2):
-        for half in range(ROWS // CHUNK):
-            rows = slice(h * ROWS + half * CHUNK, h * ROWS + (half + 1) * CHUNK)
-            qb = qc[rows, :]
-            gb = gc[rows, :]
-            lanes = slice(half * CHUNK, (half + 1) * CHUNK)
-            pl_row = plim[:1, lanes]
-            ll_row = llim[:1, lanes]
-            chunks = PKEYS // CHUNK + half + 1
-            total = jnp.zeros((1, CHUNK), jnp.float32)
-            weighted = jnp.zeros((1, CHUNK), jnp.float32)
-            for c in range(chunks):
-                cut = slice(c * CHUNK, (c + 1) * CHUNK)
-                raw = lax.dot_general(kc[cut, :], qb, NT, preferred_element_type=jnp.float32)
-                dprob = lax.dot_general(vc[cut, :], gb, NT, preferred_element_type=jnp.float32)
-                tanh_val = jnp.tanh(raw * (SCALE / SOFTCAP))
-                if c * CHUNK < PKEYS:
-                    seen = sub < pl_row - c * CHUNK
-                else:
-                    seen = sub < ll_row - (c * CHUNK - PKEYS)
-                expo = jnp.where(seen, jnp.exp(SOFTCAP * tanh_val), 0.0)
-                total = total + jnp.sum(expo, axis=0, keepdims=True)
-                weighted = weighted + jnp.sum(expo * dprob, axis=0, keepdims=True)
-                ex[cut, :] = expo
-                fx[cut, :] = expo * (1.0 - tanh_val * tanh_val)
-                dp[cut, :] = dprob
+
+    blocks = [(h, half) for h in range(2) for half in range(ROWS // CHUNK)]
+    count = [PKEYS // CHUNK + half + 1 for h, half in blocks]
+    sums = {}
+
+    def scores(n, c):
+        h, half = blocks[n]
+        rows = slice(h * ROWS + half * CHUNK, h * ROWS + (half + 1) * CHUNK)
+        cut = slice(c * CHUNK, (c + 1) * CHUNK)
+        raw = lax.dot_general(kc[cut, :], qc[rows, :], NT, preferred_element_type=jnp.float32)
+        dprob = lax.dot_general(vc[cut, :], gc[rows, :], NT, preferred_element_type=jnp.float32)
+        tanh_val = jnp.tanh(raw * (SCALE / SOFTCAP))
+        expo = jnp.exp2(tanh_val * (SOFTCAP * LOG2E)) * seen[cut, half * CHUNK : (half + 1) * CHUNK]
+        total, weighted = sums.get(n, (0.0, 0.0))
+        total = total + jnp.sum(expo, axis=0, keepdims=True)
+        weighted = weighted + jnp.sum(expo * dprob, axis=0, keepdims=True)
+        sums[n] = (total, weighted)
+        ex[n % 2, cut, :] = expo
+        fx[n % 2, cut, :] = expo * (1.0 - tanh_val * tanh_val)
+        dp[n % 2, cut, :] = dprob
+
+    def gradients(n, c, dq_t):
+        h, half = blocks[n]
+        rows = slice(h * ROWS + half * CHUNK, h * ROWS + (half + 1) * CHUNK)
+        cut = slice(c * CHUNK, (c + 1) * CHUNK)
+        inv, delta, scaled = sums[n]
+        prob16 = (ex[n % 2, cut, :] * inv).astype(jnp.bfloat16)
+        dscore16 = (fx[n % 2, cut, :] * ((dp[n % 2, cut, :] - delta) * scaled)).astype(jnp.bfloat16)
+        dv_part = jnp.dot(prob16, gc[rows, :], preferred_element_type=jnp.float32)
+        dk_part = jnp.dot(dscore16, qc[rows, :], preferred_element_type=jnp.float32)
+        if h == 0 and (half == 0 or c == PKEYS // CHUNK + 1):
+            dvc[cut, :] = dv_part
+            dkc[cut, :] = dk_part
+        else:
+            dvc[cut, :] += dv_part
+            dkc[cut, :] += dk_part
+        return dq_t + jnp.dot(kt[:, cut], dscore16, preferred_element_type=jnp.float32)
+
+    for n in range(len(blocks) + 1):
+        if n:
+            total, weighted = sums[n - 1]
             inv = 1.0 / total
-            delta = weighted * inv
-            scaled = inv * SCALE
+            sums[n - 1] = (inv, weighted * inv, inv * SCALE)
             dq_t = jnp.zeros((HD, CHUNK), jnp.float32)
-            for c in range(chunks):
-                cut = slice(c * CHUNK, (c + 1) * CHUNK)
-                prob16 = (ex[cut, :] * inv).astype(jnp.bfloat16)
-                dscore16 = (fx[cut, :] * ((dp[cut, :] - delta) * scaled)).astype(jnp.bfloat16)
-                dv_part = jnp.dot(prob16, gb, preferred_element_type=jnp.float32)
-                dk_part = jnp.dot(dscore16, qb, preferred_element_type=jnp.float32)
-                dq_t = dq_t + jnp.dot(kt[:, cut], dscore16, preferred_element_type=jnp.float32)
-                if h == 0 and (half == 0 or c == PKEYS // CHUNK + 1):
-                    dvc[cut, :] = dv_part
-                    dkc[cut, :] = dk_part
-                else:
-                    dvc[cut, :] += dv_part
-                    dkc[cut, :] += dk_part
+        for c in range(KEYS // CHUNK):
+            if n < len(blocks) and c < count[n]:
+                scores(n, c)
+            if n and c < count[n - 1]:
+                dq_t = gradients(n - 1, c, dq_t)
+        if n:
+            h, half = blocks[n - 1]
             dq_rows = dq_t.T.astype(jnp.bfloat16)
             for j in range(CHUNK // BLK):
                 dst = rows_at(meta[ORDER + half * (CHUNK // BLK) + j])
@@ -309,12 +311,9 @@
 def attend_kernel(
     meta, q, k, v, gathered, own_a, last_a, own_b, last_b,
     dq, dk, dv, ret,
-    qs, ks, vs, gs, ps, dqs, dks, dvs, rets, sem_in, sem_out, *scratch,
+    qs, ks, vs, dqs, dks, dvs, rets, sem_in, sem_out, *scratch,
 ):
-    loads = [
-        (own_a, ps.at[0, 0]), (last_a, ps.at[0, 1]), (gathered.at[:, 0], gs.at[0]), (k, ks), (v, vs), (q, qs),
-        (own_b, ps.at[1, 0]), (last_b, ps.at[1, 1]), (gathered.at[:, 1], gs.at[1]),
-    ]
+    loads = [(k, ks), (v, vs), (q, qs)]
     loads = [pltpu.make_async_copy(src, dst, sem_in.at[i]) for i, (src, dst) in enumerate(loads)]
     for copy in loads:
         copy.start()
@@ -323,11 +322,12 @@
         (rets.at[1], ret.at[:, 1]), (dqs.at[1], dq.at[:, pl.ds(2 * HD, 2 * HD)]), (dks, dk), (dvs, dv),
     ]
     stores = [pltpu.make_async_copy(src, dst, sem_out.at[i]) for i, (src, dst) in enumerate(stores)]
+    visible(meta, scratch[-1])
+    for copy in loads:
+        copy.wait()
     for a in range(2):
-        for copy in loads[6 * a : 6 + 3 * a]:
-            copy.wait()
-        parts = [ps.at[a, i] for i in range(2)]
-        attend_head(a, meta, qs, ks, vs, gs.at[a], parts, dqs.at[a], dks, dvs, rets.at[a], scratch)
+        parts = (own_b, last_b) if a else (own_a, last_a)
+        attend_head(a, meta, qs, ks, vs, gathered.at[:, a], parts, dqs.at[a], dks, dvs, rets.at[a], scratch)
         for copy in stores[2 * a : 2 + 4 * a]:
             copy.start()
     for copy in stores:
@@ -343,19 +343,17 @@
             jax.ShapeDtypeStruct(values.shape, jnp.bfloat16),
             jax.ShapeDtypeStruct(gathered.shape, jnp.bfloat16),
         ),
-        in_specs=specs(SMEM, 1) + specs(pl.ANY, 8),
+        in_specs=specs(SMEM, 1) + specs(HBM, 3) + specs(VMEM, 5),
         out_specs=tuple(specs(pl.ANY, 4)),
         scratch_shapes=[
             pltpu.VMEM(queries.shape, jnp.bfloat16),
             pltpu.VMEM(keys.shape, jnp.bfloat16),
             pltpu.VMEM(values.shape, jnp.bfloat16),
-            pltpu.VMEM((2, DEVS, PCAP * BLK, 2 * HD), jnp.bfloat16),
-            pltpu.VMEM((2, 2, ROWS, 2 * HD), jnp.bfloat16),
             pltpu.VMEM((2, ROWS, 2 * HD), jnp.bfloat16),
             pltpu.VMEM(keys.shape, jnp.bfloat16),
             pltpu.VMEM(values.shape, jnp.bfloat16),
             pltpu.VMEM((2, DEVS, PCAP * BLK, 2 * HD), jnp.bfloat16),
-            pltpu.SemaphoreType.DMA((9,)),
+            pltpu.SemaphoreType.DMA((3,)),
             pltpu.SemaphoreType.DMA((6,)),
             pltpu.VMEM((KEYS, HD), jnp.bfloat16),
             pltpu.VMEM((KEYS, HD), jnp.bfloat16),
@@ -365,11 +363,12 @@
             pltpu.VMEM((ROWS, 2 * HD), jnp.bfloat16),
             pltpu.VMEM((KEYS, HD), jnp.float32),
             pltpu.VMEM((KEYS, HD), jnp.float32),
-            pltpu.VMEM((KEYS, CHUNK), jnp.float32),
-            pltpu.VMEM((KEYS, CHUNK), jnp.float32),
-            pltpu.VMEM((KEYS, CHUNK), jnp.float32),
+            pltpu.VMEM((2, KEYS, CHUNK), jnp.float32),
+            pltpu.VMEM((2, KEYS, CHUNK), jnp.float32),
+            pltpu.VMEM((2, KEYS, CHUNK), jnp.float32),
+            pltpu.VMEM((KEYS, ROWS), jnp.float32),
         ],
-        compiler_params=params(LIM),
+        compiler_params=params(32),
         cost_estimate=pl.CostEstimate(flops=4 * 10**9, bytes_accessed=8 * 2**20, transcendentals=6 * 10**6),
         name="attend",
     )(meta, queries, keys, values, gathered, *parts)
@@ -420,9 +419,14 @@
     send_a, keep_a, send_b, keep_b = project_own(z, c, out_grad, out_weight, peer)
     recv_a = lax.ppermute(send_a, "mp", pair_a)
     recv_b = lax.ppermute(send_b, "mp", pair_b)
-    own_a, next_a = onward(keep_a, recv_a)
+    next_a = (keep_a[1].astype(jnp.float32) + recv_a[1].astype(jnp.float32)).astype(jnp.bfloat16)
+    next_b = (keep_b[1].astype(jnp.float32) + recv_b[1].astype(jnp.float32)).astype(jnp.bfloat16)
+    keep_a, recv_a, keep_b, recv_b, next_a, next_b = lax.optimization_barrier(
+        (keep_a, recv_a, keep_b, recv_b, next_a, next_b)
+    )
+    own_a = (keep_a[0].astype(jnp.float32) + recv_a[0].astype(jnp.float32)).astype(jnp.bfloat16)
+    own_b = (keep_b[0].astype(jnp.float32) + recv_b[0].astype(jnp.float32)).astype(jnp.bfloat16)
     last_a = lax.ppermute(next_a, "mp", pair_b)
-    own_b, next_b = onward(keep_b, recv_b)
     last_b = lax.ppermute(next_b, "mp", pair_a)
     parts = (own_a, last_a, own_b, last_b)
     dq, own_k, own_v, ret = attend(meta, query_states, key_states, value_states, gathered, parts)

time: 102 us -> 98 us (0.961)
  other arithmetic: 0 us -> 4.59 us
  Pallas kernels: 30.6 us -> 26.1 us
  local copies, waits for them, and re-layouts: 3.75 us -> 1.05 us
    convert_element_type x0 -> x3, other arithmetic: none -> 4.59 us  [the longest x1 1.71 us: shards(): (keep_a[1].astype(jnp.float32) + recv_a[1].astype(jnp.float32)).astype(jn...]
    pallas_call x1, Pallas kernels: 16.3 us -> 12.2 us  [attend(): pl.pallas_call(attend_kernel, out_shape=(jax.ShapeDtypeStruct(queries.sha...]
    unnamed x20 -> x8, local copies, waits for them, and re-layouts: 3.75 us -> 1.05 us
    all_to_all x1, waiting for transfers between devices: 6.73 us -> 5.18 us  [shards(): gathered = lax.all_to_all(prompt, 'seq', 0, 0, tiled=True)]
    ppermute x1, starting transfers between devices: 3.94 us -> 2.9 us  [shards(): last_a = lax.ppermute(next_a, 'mp', pair_b)]
  transfers between devices with their start and end apart: 6 -> 6, of which waited for: 3 -> 4; matrix products, arithmetic and copies ran while one was open for 0% -> 5% of each run, Pallas kernels for 6% -> 6%
where the time goes in v3:
time: 98 us; the launch traced here: 97.5 us
  blocking collectives  33 us (34%)
  Pallas kernels  26.1 us (27%)
  waiting for transfers between devices  17.4 us (18%)
  starting transfers between devices  14.6 us (15%)
  other arithmetic  4.59 us (5%)
  local copies, waits for them, and re-layouts  1.05 us (1%)
    all_to_all x1, blocking collectives, shards(): ret = lax.all_to_all(ret, 'seq', 0, 0, tiled=True)  33 us
    pallas_call x1, Pallas kernels, attend(): pl.pallas_call(attend_kernel, out_shape=(jax.ShapeDtypeStruct(queries.sha...  12.2 us
    ppermute x1, waiting for transfers between devices, shards(): recv_a = lax.ppermute(send_a, 'mp', pair_a)  9.98 us
    all_to_all x1, starting transfers between devices, shards(): gathered = lax.all_to_all(prompt, 'seq', 0, 0, tiled=True)  7.12 us
    pallas_call x1, Pallas kernels, project_peer(): pl.pallas_call(project_peer_kernel, out_shape=(jax.ShapeDtypeStruct((4, r...  6.24 us
    pallas_call x1, Pallas kernels, project_own(): pl.pallas_call(project_own_kernel, out_shape=(part, part, part, part), gr...  5.98 us
    all_to_all x1, waiting for transfers between devices, shards(): gathered = lax.all_to_all(prompt, 'seq', 0, 0, tiled=True)  5.18 us
    ppermute x1, starting transfers between devices, shards(): last_a = lax.ppermute(next_a, 'mp', pair_b)  2.9 us
  transfers between devices with their start and end apart: 6, of which 4 were waited for; matrix products, arithmetic and copies ran while one was open for 5% of the time, Pallas kernels for 6%

profile of v3, /device:TPU:0, one launch (start us, length us, event | category | flops | bytes accessed | tf_op | source)
XLA Modules:
  0.0 97.5 jit_solution(6024992352530658058)
XLA Ops:
  0.6 6.2 %project_peer.1 = (bf16[4,512,512]{2,1,0:T(8,128)(2,1)}, s32[48]{0:T(128)}, bf16[16,2,128,256]{3,2,1,0:T(8,128)(2,1)}) custom-call(s32[1]{0:T(128)} %bitcast.z, s32[1]{0:T(128)} %bitcast.1.c, s32[1]{0:T(128)} %bitcast.2.here, bf16[576,512]{1,0:T(8,128)(2,1)} %bitcast.15, bf16[576,4096]{1,0:T(8,128)(2,1)} %bitcast.13, s32[128]{0:T(128)} %seq.1, s32[128]{0:T(128)} %pos.1, ...), custom_call_target="tpu_custom_call" | custom-call | flops 1207959552 | bytes 5242880 | tf_op jit(solution)/shard_map/project_peer/pallas_call | solution.py:122
  6.9 0.1 collective-permute-start
  7.0 7.1 %all-to-all-start = ((bf16[16,2,128,256]{3,2,1,0:T(8,128)(2,1)}), bf16[16,2,128,256]{3,2,1,0:T(8,128)(2,1)S(1)}, u32[]{:S(2)}, u32[]{:S(2)}) async-start(bf16[16,2,128,256]{3,2,1,0:T(8,128)(2,1)} %get-tuple-element.23), calls=%async_computation | async-start | bytes 4194304 | tf_op jit(solution)/shard_map/all_to_all | solution.py:418
  14.1 0.0 collective-permute-done.peer
  14.1 6.0 %project_own.1 = (bf16[2,512,256]{2,1,0:T(8,128)(2,1)}, bf16[2,512,256]{2,1,0:T(8,128)(2,1)}, bf16[2,512,256]{2,1,0:T(8,128)(2,1)}, bf16[2,512,256]{2,1,0:T(8,128)(2,1)}) custom-call(s32[1]{0:T(128)} %bitcast.z, s32[1]{0:T(128)} %bitcast.1.c, bf16[576,512]{1,0:T(8,128)(2,1)} %bitcast.16, bf16[576,4096]{1,0:T(8,128)(2,1)} %bitcast.14, ...), custom_call_target="tpu_custom_call" | custom-call | flops 1207959552 | bytes 7340032 | tf_op jit(solution)/shard_map/project_own/pallas_call | solution.py:184
  20.1 0.0 copy-start
  20.1 0.0 copy-start.1
  20.1 0.0 copy-start.2
  20.1 2.0 %collective-permute-start.1 = (bf16[2,512,256]{2,1,0:T(8,128)(2,1)}, bf16[2,512,256]{2,1,0:T(8,128)(2,1)S(1)}, u32[]{:S(2)}, u32[]{:S(2)}) collective-permute-start(bf16[2,512,256]{2,1,0:T(8,128)(2,1)} %get-tuple-element.26), channel_id=1, source_target_pairs={{0,2},{2,0},{4,6},{6,4},{1,3},{3,1},{5,7},{7,5},{8,10},{10,8},{12,... | collective-permute-start | bytes 1572872 | tf_op jit(solution)/shard_map/ppermute | solution.py:420
  22.1 2.5 %collective-permute-start.2 = (bf16[2,512,256]{2,1,0:T(8,128)(2,1)}, bf16[2,512,256]{2,1,0:T(8,128)(2,1)S(1)}, u32[]{:S(2)}, u32[]{:S(2)}) collective-permute-start(bf16[2,512,256]{2,1,0:T(8,128)(2,1)} %get-tuple-element.28), channel_id=1, source_target_pairs={{0,6},{2,4},{4,2},{6,0},{1,7},{3,5},{5,3},{7,1},{8,14},{10,12},{12... | collective-permute-start | bytes 1572872 | tf_op jit(solution)/shard_map/ppermute | solution.py:421
  24.6 10.0 %collective-permute-done.1 = bf16[2,512,256]{2,1,0:T(8,128)(2,1)S(1)} collective-permute-done((bf16[2,512,256]{2,1,0:T(8,128)(2,1)}, bf16[2,512,256]{2,1,0:T(8,128)(2,1)S(1)}, u32[]{:S(2)}, u32[]{:S(2)}) %collective-permute-start.1) | collective-permute-done | bytes 524320 | tf_op jit(solution)/shard_map/ppermute | solution.py:420
  34.6 1.7 %fusion = bf16[512,256]{1,0:T(8,128)(2,1)} fusion(bf16[2,512,256]{2,1,0:T(8,128)(2,1)S(1)} %collective-permute-done.1, bf16[2,512,256]{2,1,0:T(8,128)(2,1)} %get-tuple-element.29), kind=kLoop, calls=%fused_computation.4 | loop fusion | flops 524288 | bytes 786432 | tf_op jit(solution)/shard_map/convert_element_type | solution.py:422
  36.3 1.0 collective-permute-done.2
  37.3 1.7 %fusion.1 = bf16[512,256]{1,0:T(8,128)(2,1)} fusion(bf16[2,512,256]{2,1,0:T(8,128)(2,1)S(1)} %collective-permute-done.2, bf16[2,512,256]{2,1,0:T(8,128)(2,1)} %get-tuple-element.32), kind=kLoop, calls=%fused_computation.5 | loop fusion | flops 524288 | bytes 786432 | tf_op jit(solution)/shard_map/convert_element_type | solution.py:423
  39.0 2.9 %collective-permute-start.3 = (bf16[512,256]{1,0:T(8,128)(2,1)}, bf16[512,256]{1,0:T(8,128)(2,1)S(1)}, u32[]{:S(2)}, u32[]{:S(2)}) collective-permute-start(bf16[512,256]{1,0:T(8,128)(2,1)} %fusion), channel_id=1, source_target_pairs={{0,6},{2,4},{4,2},{6,0},{1,7},{3,5},{5,3},{7,1},{8,14},{10,12},{12... | collective-permute-start | bytes 786440 | tf_op jit(solution)/shard_map/ppermute | solution.py:429
  41.9 0.0 collective-permute-start.4
  41.9 1.2 %fusion.2 = (bf16[512,256]{1,0:T(8,128)(2,1)S(1)}, bf16[512,256]{1,0:T(8,128)(2,1)S(1)}) fusion(bf16[2,512,256]{2,1,0:T(8,128)(2,1)S(1)} %collective-permute-done.1, bf16[2,512,256]{2,1,0:T(8,128)(2,1)} %get-tuple-element.29, bf16[2,512,256]{2,1,0:T(8,128)(2,1)S(1)} %collective-permute-done.2, bf16[2,512,256]{2,1,0:T(8,128)(2,1)} %get-tuple-element.32), kind=kLoop, calls=%fused_computation.6 | loop fusion | flops 1048576 | bytes 1572864 | tf_op jit(solution)/shard_map/convert_element_type | solution.py:427
  43.1 5.2 %all-to-all-done.gathered = bf16[16,2,128,256]{3,2,1,0:T(8,128)(2,1)S(1)} async-done(((bf16[16,2,128,256]{3,2,1,0:T(8,128)(2,1)}), bf16[16,2,128,256]{3,2,1,0:T(8,128)(2,1)S(1)}, u32[]{:S(2)}, u32[]{:S(2)}) %all-to-all-start) | async-done | bytes 2097184 | tf_op jit(solution)/shard_map/all_to_all | solution.py:418
  48.3 0.0 collective-permute-done.3.last_a
  48.3 1.3 %collective-permute-done.4.last_b = bf16[512,256]{1,0:T(8,128)(2,1)} collective-permute-done((bf16[512,256]{1,0:T(8,128)(2,1)}, bf16[512,256]{1,0:T(8,128)(2,1)}, u32[]{:S(2)}, u32[]{:S(2)}) %collective-permute-start.4) | collective-permute-done | bytes 262176 | tf_op jit(solution)/shard_map/ppermute | solution.py:430
  49.5 0.0 copy-done
  49.5 0.0 copy-done.1
  49.5 0.0 copy-done.2
  49.5 0.0 copy-start.3
  49.6 1.0 %copy-done.3 = bf16[512,512]{1,0:T(8,128)(2,1)S(1)} copy-done((bf16[512,512]{1,0:T(8,128)(2,1)S(1)}, bf16[512,512]{1,0:T(8,128)(2,1)}, u32[]{:S(2)}) %copy-start.3) | copy-done | bytes 524312
  50.6 12.2 %attend.1 = (bf16[512,512]{1,0:T(8,128)(2,1)}, bf16[512,256]{1,0:T(8,128)(2,1)S(1)}, bf16[512,256]{1,0:T(8,128)(2,1)S(1)}, bf16[16,2,128,256]{3,2,1,0:T(8,128)(2,1)S(1)}) custom-call(s32[48]{0:T(128)S(1)} %copy-done.2, bf16[512,512]{1,0:T(8,128)(2,1)S(1)} %copy-done.3, bf16[512,256]{1,0:T(8,128)(2,1)S(1)} %copy-done, bf16[512,256]{1,0:T(8,128)(2,1)S(1)} %copy-done.1, ...), custom_call_target="tpu_custom_call" | custom-call | flops 4000000000 | bytes 8388608 | tf_op jit(solution)/shard_map/attend/pallas_call | solution.py:338
  62.8 33.0 %all_to_all.10.ret = bf16[16,2,128,256]{3,2,1,0:T(8,128)(2,1)S(1)} all-to-all(bf16[16,2,128,256]{3,2,1,0:T(8,128)(2,1)S(1)} %get-tuple-element.38), channel_id=1, replica_groups=mesh['seq'=16,'mp'=4,'section'=2] {'seq'}, dimensions={0} | all-to-all | bytes 4194304 | tf_op jit(solution)/shard_map/all_to_all | solution.py:433
  95.8 1.7 %finish.1 = (bf16[512,256]{1,0:T(8,128)(2,1)}, bf16[512,256]{1,0:T(8,128)(2,1)}) custom-call(s32[48]{0:T(128)S(1)} %copy-done.2, bf16[512,256]{1,0:T(8,128)(2,1)S(1)} %get-tuple-element.36.own_k, bf16[512,256]{1,0:T(8,128)(2,1)S(1)} %get-tuple-element.37.own_v, bf16[16,2,128,256]{3,2,1,0:T(8,128)(2,1)S(1)} %all_to_all.10.ret), custom_call_target="tpu_custom_call" | custom-call | tf_op jit(solution)/shard_map/finish/pallas_call | solution.py:395
Async XLA Ops:
  6.9 7.2 %collective-permute-start = (bf16[4,512,512]{2,1,0:T(8,128)(2,1)}, bf16[4,512,512]{2,1,0:T(8,128)(2,1)}, u32[]{:S(2)}, u32[]{:S(2)}) collective-permute-start(bf16[4,512,512]{2,1,0:T(8,128)(2,1)} %get-tuple-element.24), channel_id=1, source_target_pairs={{0,1},{1,0},{2,3},{3,2},{4,5},{5,4},{6,7},{7,6},{8,9},{9,8},{10,11... | collective-permute-start | bytes 6291464 | tf_op jit(solution)/shard_map/ppermute | solution.py:417
  7.0 41.3 %all-to-all-start = ((bf16[16,2,128,256]{3,2,1,0:T(8,128)(2,1)}), bf16[16,2,128,256]{3,2,1,0:T(8,128)(2,1)S(1)}, u32[]{:S(2)}, u32[]{:S(2)}) async-start(bf16[16,2,128,256]{3,2,1,0:T(8,128)(2,1)} %get-tuple-element.23), calls=%async_computation | async-start | bytes 4194304 | tf_op jit(solution)/shard_map/all_to_all | solution.py:418
  20.1 29.4 %copy-start = (bf16[512,256]{1,0:T(8,128)(2,1)S(1)}, bf16[512,256]{1,0:T(8,128)(2,1)}, u32[]{:S(2)}) copy-start(bf16[512,256]{1,0:T(8,128)(2,1)} %k.1) | copy-start | bytes 786436
  20.1 29.4 %copy-start.1 = (bf16[512,256]{1,0:T(8,128)(2,1)S(1)}, bf16[512,256]{1,0:T(8,128)(2,1)}, u32[]{:S(2)}) copy-start(bf16[512,256]{1,0:T(8,128)(2,1)} %v.1) | copy-start | bytes 786436
  20.1 29.4 %copy-start.2 = (s32[48]{0:T(128)S(1)}, s32[48]{0:T(128)}, u32[]{:S(2)}) copy-start(s32[48]{0:T(128)} %get-tuple-element.22.meta) | copy-start | bytes 580
  20.1 14.5 %collective-permute-start.1 = (bf16[2,512,256]{2,1,0:T(8,128)(2,1)}, bf16[2,512,256]{2,1,0:T(8,128)(2,1)S(1)}, u32[]{:S(2)}, u32[]{:S(2)}) collective-permute-start(bf16[2,512,256]{2,1,0:T(8,128)(2,1)} %get-tuple-element.26), channel_id=1, source_target_pairs={{0,2},{2,0},{4,6},{6,4},{1,3},{3,1},{5,7},{7,5},{8,10},{10,8},{12,... | collective-permute-start | bytes 1572872 | tf_op jit(solution)/shard_map/ppermute | solution.py:420
  22.1 15.2 %collective-permute-start.2 = (bf16[2,512,256]{2,1,0:T(8,128)(2,1)}, bf16[2,512,256]{2,1,0:T(8,128)(2,1)S(1)}, u32[]{:S(2)}, u32[]{:S(2)}) collective-permute-start(bf16[2,512,256]{2,1,0:T(8,128)(2,1)} %get-tuple-element.28), channel_id=1, source_target_pairs={{0,6},{2,4},{4,2},{6,0},{1,7},{3,5},{5,3},{7,1},{8,14},{10,12},{12... | collective-permute-start | bytes 1572872 | tf_op jit(solution)/shard_map/ppermute | solution.py:421
  39.0 9.3 %collective-permute-start.3 = (bf16[512,256]{1,0:T(8,128)(2,1)}, bf16[512,256]{1,0:T(8,128)(2,1)S(1)}, u32[]{:S(2)}, u32[]{:S(2)}) collective-permute-start(bf16[512,256]{1,0:T(8,128)(2,1)} %fusion), channel_id=1, source_target_pairs={{0,6},{2,4},{4,2},{6,0},{1,7},{3,5},{5,3},{7,1},{8,14},{10,12},{12... | collective-permute-start | bytes 786440 | tf_op jit(solution)/shard_map/ppermute | solution.py:429
  41.9 7.6 %collective-permute-start.4 = (bf16[512,256]{1,0:T(8,128)(2,1)}, bf16[512,256]{1,0:T(8,128)(2,1)}, u32[]{:S(2)}, u32[]{:S(2)}) collective-permute-start(bf16[512,256]{1,0:T(8,128)(2,1)} %fusion.1), channel_id=1, source_target_pairs={{0,2},{2,0},{4,6},{6,4},{1,3},{3,1},{5,7},{7,5},{8,10},{10,8},{12,... | collective-permute-start | bytes 786440 | tf_op jit(solution)/shard_map/ppermute | solution.py:430
  49.5 1.0 %copy-start.3 = (bf16[512,512]{1,0:T(8,128)(2,1)S(1)}, bf16[512,512]{1,0:T(8,128)(2,1)}, u32[]{:S(2)}) copy-start(bf16[512,512]{1,0:T(8,128)(2,1)} %q.1) | copy-start | bytes 1572868

commit v4 on v3

--- a/solution.py
+++ b/solution.py
@@ -51,6 +51,9 @@
 
 def place(slot):
     return lax.shift_right_logical(slot, 1), rows_at(slot & 1)
+
+
+BACK = tuple(range(DEVS - 1, -1, -1))
 
 
 def make_layout(here, seq, pos, depth, keys, values, meta, block):
@@ -298,6 +301,7 @@
     ret[...] = jnp.zeros(ret.shape, ret.dtype)
     for p in range(16):
         dev, dst = place(meta[PLIST + p])
+        dev = DEVS - 1 - dev
         src = slice(p * BLK, (p + 1) * BLK)
         ret[dev, dst, :HD] = dkc[src, :].astype(jnp.bfloat16)
         ret[dev, dst, HD:] = dvc[src, :].astype(jnp.bfloat16)
@@ -430,7 +434,7 @@
     last_b = lax.ppermute(next_b, "mp", pair_a)
     parts = (own_a, last_a, own_b, last_b)
     dq, own_k, own_v, ret = attend(meta, query_states, key_states, value_states, gathered, parts)
-    ret = lax.all_to_all(ret, "seq", 0, 0, tiled=True)
+    ret = lax.all_to_all(ret, "seq", 0, 0, tiled=True, axis_index_groups=[list(BACK)])
     dk, dv = finish(meta, own_k, own_v, ret)
     return dq, dk, dv
 

time: 98 us -> 95.5 us (0.974)
  blocking collectives: 33 us -> 30.6 us
    all_to_all x1, blocking collectives: 33 us -> 30.6 us  [shards(): lax.all_to_all(ret, 'seq', 0, 0, tiled=True, axis_index_groups=[list(BACK)])]
where the time goes in v4:
time: 95.5 us; the launch traced here: 94.9 us
  blocking collectives  30.6 us (32%)
  Pallas kernels  25.9 us (27%)
  waiting for transfers between devices  17.4 us (18%)
  starting transfers between devices  14.6 us (15%)
  other arithmetic  4.59 us (5%)
  local copies, waits for them, and re-layouts  1.05 us (1%)
    all_to_all x1, blocking collectives, shards(): lax.all_to_all(ret, 'seq', 0, 0, tiled=True, axis_index_groups=[list(BACK)])  30.6 us
    pallas_call x1, Pallas kernels, attend(): pl.pallas_call(attend_kernel, out_shape=(jax.ShapeDtypeStruct(queries.sha...  12.2 us
    ppermute x1, waiting for transfers between devices, shards(): recv_a = lax.ppermute(send_a, 'mp', pair_a)  9.98 us
    all_to_all x1, starting transfers between devices, shards(): gathered = lax.all_to_all(prompt, 'seq', 0, 0, tiled=True)  7.13 us
    pallas_call x1, Pallas kernels, project_peer(): pl.pallas_call(project_peer_kernel, out_shape=(jax.ShapeDtypeStruct((4, r...  6.22 us
    pallas_call x1, Pallas kernels, project_own(): pl.pallas_call(project_own_kernel, out_shape=(part, part, part, part), gr...  5.99 us
    all_to_all x1, waiting for transfers between devices, shards(): gathered = lax.all_to_all(prompt, 'seq', 0, 0, tiled=True)  5.19 us
    ppermute x1, starting transfers between devices, shards(): last_a = lax.ppermute(next_a, 'mp', pair_b)  2.91 us
  transfers between devices with their start and end apart: 6, of which 4 were waited for; matrix products, arithmetic and copies ran while one was open for 5% of the time, Pallas kernels for 6%

profile of v4, /device:TPU:0, one launch (start us, length us, event | category | flops | bytes accessed | tf_op | source)
XLA Modules:
  0.0 94.9 jit_solution(11056008602626160639)
XLA Ops:
  0.6 6.2 %project_peer.1 = (bf16[4,512,512]{2,1,0:T(8,128)(2,1)}, s32[48]{0:T(128)}, bf16[16,2,128,256]{3,2,1,0:T(8,128)(2,1)}) custom-call(s32[1]{0:T(128)} %bitcast.z, s32[1]{0:T(128)} %bitcast.1.c, s32[1]{0:T(128)} %bitcast.2.here, bf16[576,512]{1,0:T(8,128)(2,1)} %bitcast.15, bf16[576,4096]{1,0:T(8,128)(2,1)} %bitcast.13, s32[128]{0:T(128)} %seq.1, s32[128]{0:T(128)} %pos.1, ...), custom_call_target="tpu_custom_call" | custom-call | flops 1207959552 | bytes 5242880 | tf_op jit(solution)/shard_map/project_peer/pallas_call | solution.py:125
  6.9 0.1 collective-permute-start
  7.0 7.1 %all-to-all-start = ((bf16[16,2,128,256]{3,2,1,0:T(8,128)(2,1)}), bf16[16,2,128,256]{3,2,1,0:T(8,128)(2,1)S(1)}, u32[]{:S(2)}, u32[]{:S(2)}) async-start(bf16[16,2,128,256]{3,2,1,0:T(8,128)(2,1)} %get-tuple-element.23), calls=%async_computation | async-start | bytes 4194304 | tf_op jit(solution)/shard_map/all_to_all | solution.py:422
  14.1 0.0 collective-permute-done.peer
  14.1 6.0 %project_own.1 = (bf16[2,512,256]{2,1,0:T(8,128)(2,1)}, bf16[2,512,256]{2,1,0:T(8,128)(2,1)}, bf16[2,512,256]{2,1,0:T(8,128)(2,1)}, bf16[2,512,256]{2,1,0:T(8,128)(2,1)}) custom-call(s32[1]{0:T(128)} %bitcast.z, s32[1]{0:T(128)} %bitcast.1.c, bf16[576,512]{1,0:T(8,128)(2,1)} %bitcast.16, bf16[576,4096]{1,0:T(8,128)(2,1)} %bitcast.14, ...), custom_call_target="tpu_custom_call" | custom-call | flops 1207959552 | bytes 7340032 | tf_op jit(solution)/shard_map/project_own/pallas_call | solution.py:187
  20.1 0.0 copy-start
  20.1 0.0 copy-start.1
  20.1 0.0 copy-start.2
  20.1 2.0 %collective-permute-start.1 = (bf16[2,512,256]{2,1,0:T(8,128)(2,1)}, bf16[2,512,256]{2,1,0:T(8,128)(2,1)S(1)}, u32[]{:S(2)}, u32[]{:S(2)}) collective-permute-start(bf16[2,512,256]{2,1,0:T(8,128)(2,1)} %get-tuple-element.26), channel_id=1, source_target_pairs={{0,2},{2,0},{4,6},{6,4},{1,3},{3,1},{5,7},{7,5},{8,10},{10,8},{12,... | collective-permute-start | bytes 1572872 | tf_op jit(solution)/shard_map/ppermute | solution.py:424
  22.1 2.5 %collective-permute-start.2 = (bf16[2,512,256]{2,1,0:T(8,128)(2,1)}, bf16[2,512,256]{2,1,0:T(8,128)(2,1)S(1)}, u32[]{:S(2)}, u32[]{:S(2)}) collective-permute-start(bf16[2,512,256]{2,1,0:T(8,128)(2,1)} %get-tuple-element.28), channel_id=1, source_target_pairs={{0,6},{2,4},{4,2},{6,0},{1,7},{3,5},{5,3},{7,1},{8,14},{10,12},{12... | collective-permute-start | bytes 1572872 | tf_op jit(solution)/shard_map/ppermute | solution.py:425
  24.6 10.0 %collective-permute-done.1 = bf16[2,512,256]{2,1,0:T(8,128)(2,1)S(1)} collective-permute-done((bf16[2,512,256]{2,1,0:T(8,128)(2,1)}, bf16[2,512,256]{2,1,0:T(8,128)(2,1)S(1)}, u32[]{:S(2)}, u32[]{:S(2)}) %collective-permute-start.1) | collective-permute-done | bytes 524320 | tf_op jit(solution)/shard_map/ppermute | solution.py:424
  34.6 1.7 %fusion = bf16[512,256]{1,0:T(8,128)(2,1)} fusion(bf16[2,512,256]{2,1,0:T(8,128)(2,1)S(1)} %collective-permute-done.1, bf16[2,512,256]{2,1,0:T(8,128)(2,1)} %get-tuple-element.29), kind=kLoop, calls=%fused_computation.4 | loop fusion | flops 524288 | bytes 786432 | tf_op jit(solution)/shard_map/convert_element_type | solution.py:426
  36.3 1.0 %collective-permute-done.2 = bf16[2,512,256]{2,1,0:T(8,128)(2,1)S(1)} collective-permute-done((bf16[2,512,256]{2,1,0:T(8,128)(2,1)}, bf16[2,512,256]{2,1,0:T(8,128)(2,1)S(1)}, u32[]{:S(2)}, u32[]{:S(2)}) %collective-permute-start.2) | collective-permute-done | bytes 524320 | tf_op jit(solution)/shard_map/ppermute | solution.py:425
  37.3 1.7 %fusion.1 = bf16[512,256]{1,0:T(8,128)(2,1)} fusion(bf16[2,512,256]{2,1,0:T(8,128)(2,1)S(1)} %collective-permute-done.2, bf16[2,512,256]{2,1,0:T(8,128)(2,1)} %get-tuple-element.32), kind=kLoop, calls=%fused_computation.5 | loop fusion | flops 524288 | bytes 786432 | tf_op jit(solution)/shard_map/convert_element_type | solution.py:427
  39.0 2.9 %collective-permute-start.3 = (bf16[512,256]{1,0:T(8,128)(2,1)}, bf16[512,256]{1,0:T(8,128)(2,1)S(1)}, u32[]{:S(2)}, u32[]{:S(2)}) collective-permute-start(bf16[512,256]{1,0:T(8,128)(2,1)} %fusion), channel_id=1, source_target_pairs={{0,6},{2,4},{4,2},{6,0},{1,7},{3,5},{5,3},{7,1},{8,14},{10,12},{12... | collective-permute-start | bytes 786440 | tf_op jit(solution)/shard_map/ppermute | solution.py:433
  41.9 0.0 collective-permute-start.4
  41.9 1.2 %fusion.2 = (bf16[512,256]{1,0:T(8,128)(2,1)S(1)}, bf16[512,256]{1,0:T(8,128)(2,1)S(1)}) fusion(bf16[2,512,256]{2,1,0:T(8,128)(2,1)S(1)} %collective-permute-done.1, bf16[2,512,256]{2,1,0:T(8,128)(2,1)} %get-tuple-element.29, bf16[2,512,256]{2,1,0:T(8,128)(2,1)S(1)} %collective-permute-done.2, bf16[2,512,256]{2,1,0:T(8,128)(2,1)} %get-tuple-element.32), kind=kLoop, calls=%fused_computation.6 | loop fusion | flops 1048576 | bytes 1572864 | tf_op jit(solution)/shard_map/convert_element_type | solution.py:431
  43.1 5.2 %all-to-all-done.gathered = bf16[16,2,128,256]{3,2,1,0:T(8,128)(2,1)S(1)} async-done(((bf16[16,2,128,256]{3,2,1,0:T(8,128)(2,1)}), bf16[16,2,128,256]{3,2,1,0:T(8,128)(2,1)S(1)}, u32[]{:S(2)}, u32[]{:S(2)}) %all-to-all-start) | async-done | bytes 2097184 | tf_op jit(solution)/shard_map/all_to_all | solution.py:422
  48.3 0.0 collective-permute-done.3.last_a
  48.3 1.3 %collective-permute-done.4.last_b = bf16[512,256]{1,0:T(8,128)(2,1)} collective-permute-done((bf16[512,256]{1,0:T(8,128)(2,1)}, bf16[512,256]{1,0:T(8,128)(2,1)}, u32[]{:S(2)}, u32[]{:S(2)}) %collective-permute-start.4) | collective-permute-done | bytes 262176 | tf_op jit(solution)/shard_map/ppermute | solution.py:434
  49.5 0.0 copy-done
  49.5 0.0 copy-done.1
  49.5 0.0 copy-done.2
  49.5 0.0 copy-start.3
  49.5 1.0 %copy-done.3 = bf16[512,512]{1,0:T(8,128)(2,1)S(1)} copy-done((bf16[512,512]{1,0:T(8,128)(2,1)S(1)}, bf16[512,512]{1,0:T(8,128)(2,1)}, u32[]{:S(2)}) %copy-start.3) | copy-done | bytes 524312
  50.6 12.2 %attend.1 = (bf16[512,512]{1,0:T(8,128)(2,1)}, bf16[512,256]{1,0:T(8,128)(2,1)S(1)}, bf16[512,256]{1,0:T(8,128)(2,1)S(1)}, bf16[16,2,128,256]{3,2,1,0:T(8,128)(2,1)S(1)}) custom-call(s32[48]{0:T(128)S(1)} %copy-done.2, bf16[512,512]{1,0:T(8,128)(2,1)S(1)} %copy-done.3, bf16[512,256]{1,0:T(8,128)(2,1)S(1)} %copy-done, bf16[512,256]{1,0:T(8,128)(2,1)S(1)} %copy-done.1, ...), custom_call_target="tpu_custom_call" | custom-call | flops 4000000000 | bytes 8388608 | tf_op jit(solution)/shard_map/attend/pallas_call | solution.py:342
  62.8 30.6 %all_to_all.10.ret = bf16[16,2,128,256]{3,2,1,0:T(8,128)(2,1)S(1)} all-to-all(bf16[16,2,128,256]{3,2,1,0:T(8,128)(2,1)S(1)} %get-tuple-element.38), channel_id=1, replica_groups={{120,112,104,96,88,80,72,64,56,48,40,32,24,16,8,0},{121,113,105,97,89,8..., dimensions={0} | all-to-all | bytes 4194304 | tf_op jit(solution)/shard_map/all_to_all | solution.py:437
  93.4 1.5 %finish.1 = (bf16[512,256]{1,0:T(8,128)(2,1)}, bf16[512,256]{1,0:T(8,128)(2,1)}) custom-call(s32[48]{0:T(128)S(1)} %copy-done.2, bf16[512,256]{1,0:T(8,128)(2,1)S(1)} %get-tuple-element.36.own_k, bf16[512,256]{1,0:T(8,128)(2,1)S(1)} %get-tuple-element.37.own_v, bf16[16,2,128,256]{3,2,1,0:T(8,128)(2,1)S(1)} %all_to_all.10.ret), custom_call_target="tpu_custom_call" | custom-call | tf_op jit(solution)/shard_map/finish/pallas_call | solution.py:399
Async XLA Ops:
  6.9 7.2 %collective-permute-start = (bf16[4,512,512]{2,1,0:T(8,128)(2,1)}, bf16[4,512,512]{2,1,0:T(8,128)(2,1)}, u32[]{:S(2)}, u32[]{:S(2)}) collective-permute-start(bf16[4,512,512]{2,1,0:T(8,128)(2,1)} %get-tuple-element.24), channel_id=1, source_target_pairs={{0,1},{1,0},{2,3},{3,2},{4,5},{5,4},{6,7},{7,6},{8,9},{9,8},{10,11... | collective-permute-start | bytes 6291464 | tf_op jit(solution)/shard_map/ppermute | solution.py:421
  7.0 41.3 %all-to-all-start = ((bf16[16,2,128,256]{3,2,1,0:T(8,128)(2,1)}), bf16[16,2,128,256]{3,2,1,0:T(8,128)(2,1)S(1)}, u32[]{:S(2)}, u32[]{:S(2)}) async-start(bf16[16,2,128,256]{3,2,1,0:T(8,128)(2,1)} %get-tuple-element.23), calls=%async_computation | async-start | bytes 4194304 | tf_op jit(solution)/shard_map/all_to_all | solution.py:422
  20.1 29.4 %copy-start = (bf16[512,256]{1,0:T(8,128)(2,1)S(1)}, bf16[512,256]{1,0:T(8,128)(2,1)}, u32[]{:S(2)}) copy-start(bf16[512,256]{1,0:T(8,128)(2,1)} %k.1) | copy-start | bytes 786436
  20.1 29.4 %copy-start.1 = (bf16[512,256]{1,0:T(8,128)(2,1)S(1)}, bf16[512,256]{1,0:T(8,128)(2,1)}, u32[]{:S(2)}) copy-start(bf16[512,256]{1,0:T(8,128)(2,1)} %v.1) | copy-start | bytes 786436
  20.1 29.4 %copy-start.2 = (s32[48]{0:T(128)S(1)}, s32[48]{0:T(128)}, u32[]{:S(2)}) copy-start(s32[48]{0:T(128)} %get-tuple-element.22.meta) | copy-start | bytes 580
  20.1 14.5 %collective-permute-start.1 = (bf16[2,512,256]{2,1,0:T(8,128)(2,1)}, bf16[2,512,256]{2,1,0:T(8,128)(2,1)S(1)}, u32[]{:S(2)}, u32[]{:S(2)}) collective-permute-start(bf16[2,512,256]{2,1,0:T(8,128)(2,1)} %get-tuple-element.26), channel_id=1, source_target_pairs={{0,2},{2,0},{4,6},{6,4},{1,3},{3,1},{5,7},{7,5},{8,10},{10,8},{12,... | collective-permute-start | bytes 1572872 | tf_op jit(solution)/shard_map/ppermute | solution.py:424
  22.1 15.2 %collective-permute-start.2 = (bf16[2,512,256]{2,1,0:T(8,128)(2,1)}, bf16[2,512,256]{2,1,0:T(8,128)(2,1)S(1)}, u32[]{:S(2)}, u32[]{:S(2)}) collective-permute-start(bf16[2,512,256]{2,1,0:T(8,128)(2,1)} %get-tuple-element.28), channel_id=1, source_target_pairs={{0,6},{2,4},{4,2},{6,0},{1,7},{3,5},{5,3},{7,1},{8,14},{10,12},{12... | collective-permute-start | bytes 1572872 | tf_op jit(solution)/shard_map/ppermute | solution.py:425
  39.0 9.3 %collective-permute-start.3 = (bf16[512,256]{1,0:T(8,128)(2,1)}, bf16[512,256]{1,0:T(8,128)(2,1)S(1)}, u32[]{:S(2)}, u32[]{:S(2)}) collective-permute-start(bf16[512,256]{1,0:T(8,128)(2,1)} %fusion), channel_id=1, source_target_pairs={{0,6},{2,4},{4,2},{6,0},{1,7},{3,5},{5,3},{7,1},{8,14},{10,12},{12... | collective-permute-start | bytes 786440 | tf_op jit(solution)/shard_map/ppermute | solution.py:433
  41.9 7.6 %collective-permute-start.4 = (bf16[512,256]{1,0:T(8,128)(2,1)}, bf16[512,256]{1,0:T(8,128)(2,1)}, u32[]{:S(2)}, u32[]{:S(2)}) collective-permute-start(bf16[512,256]{1,0:T(8,128)(2,1)} %fusion.1), channel_id=1, source_target_pairs={{0,2},{2,0},{4,6},{6,4},{1,3},{3,1},{5,7},{7,5},{8,10},{10,8},{12,... | collective-permute-start | bytes 786440 | tf_op jit(solution)/shard_map/ppermute | solution.py:434
  49.5 1.0 %copy-start.3 = (bf16[512,512]{1,0:T(8,128)(2,1)S(1)}, bf16[512,512]{1,0:T(8,128)(2,1)}, u32[]{:S(2)}) copy-start(bf16[512,512]{1,0:T(8,128)(2,1)} %q.1) | copy-start | bytes 1572868

commit v5 on v3

--- a/solution.py
+++ b/solution.py
@@ -51,6 +51,9 @@
 
 def place(slot):
     return lax.shift_right_logical(slot, 1), rows_at(slot & 1)
+
+
+KEYS_ORDER, BACK_ORDER = 0, 10
 
 
 def make_layout(here, seq, pos, depth, keys, values, meta, block):
@@ -227,6 +230,7 @@
     cols = slice(a * HD, (a + 1) * HD)
     for p in range(16):
         dev, src = place(meta[PLIST + p])
+        dev = dev ^ KEYS_ORDER
         kc[p * BLK : (p + 1) * BLK, :] = gathered[dev, src, :HD]
         vc[p * BLK : (p + 1) * BLK, :] = gathered[dev, src, HD:]
 
@@ -298,6 +302,7 @@
     ret[...] = jnp.zeros(ret.shape, ret.dtype)
     for p in range(16):
         dev, dst = place(meta[PLIST + p])
+        dev = dev ^ BACK_ORDER
         src = slice(p * BLK, (p + 1) * BLK)
         ret[dev, dst, :HD] = dkc[src, :].astype(jnp.bfloat16)
         ret[dev, dst, HD:] = dvc[src, :].astype(jnp.bfloat16)
@@ -415,7 +420,7 @@
     slots = (slot_seq, slot_pos, fork_depth)
     peer, meta, prompt = project_peer(z, c, here, out_grad, out_weight, *slots, key_states, value_states)
     peer = lax.ppermute(peer, "section", [(0, 1), (1, 0)])
-    gathered = lax.all_to_all(prompt, "seq", 0, 0, tiled=True)
+    gathered = lax.all_to_all(prompt, "seq", 0, 0, tiled=True, axis_index_groups=[[i ^ KEYS_ORDER for i in range(DEVS)]])
     send_a, keep_a, send_b, keep_b = project_own(z, c, out_grad, out_weight, peer)
     recv_a = lax.ppermute(send_a, "mp", pair_a)
     recv_b = lax.ppermute(send_b, "mp", pair_b)
@@ -430,7 +435,7 @@
     last_b = lax.ppermute(next_b, "mp", pair_a)
     parts = (own_a, last_a, own_b, last_b)
     dq, own_k, own_v, ret = attend(meta, query_states, key_states, value_states, gathered, parts)
-    ret = lax.all_to_all(ret, "seq", 0, 0, tiled=True)
+    ret = lax.all_to_all(ret, "seq", 0, 0, tiled=True, axis_index_groups=[[i ^ BACK_ORDER for i in range(DEVS)]])
     dk, dv = finish(meta, own_k, own_v, ret)
     return dq, dk, dv
 

time: 98 us -> 94.6 us (0.965)
  blocking collectives: 33 us -> 29.7 us
    all_to_all x1, blocking collectives: 33 us -> 29.7 us  [shards(): lax.all_to_all(ret, 'seq', 0, 0, tiled=True, axis_index_groups=[[i ^ BACK...]
where the time goes in v5:
time: 94.6 us; the launch traced here: 94.1 us
  blocking collectives  29.7 us (31%)
  Pallas kernels  26.1 us (28%)
  waiting for transfers between devices  17.4 us (18%)
  starting transfers between devices  14.6 us (15%)
  other arithmetic  4.59 us (5%)
  local copies, waits for them, and re-layouts  1.05 us (1%)
    all_to_all x1, blocking collectives, shards(): lax.all_to_all(ret, 'seq', 0, 0, tiled=True, axis_index_groups=[[i ^ BACK...  29.7 us
    pallas_call x1, Pallas kernels, attend(): pl.pallas_call(attend_kernel, out_shape=(jax.ShapeDtypeStruct(queries.sha...  12.2 us
    ppermute x1, waiting for transfers between devices, shards(): recv_a = lax.ppermute(send_a, 'mp', pair_a)  9.99 us
    all_to_all x1, starting transfers between devices, shards(): lax.all_to_all(prompt, 'seq', 0, 0, tiled=True, axis_index_groups=[[i ^ K...  7.13 us
    pallas_call x1, Pallas kernels, project_peer(): pl.pallas_call(project_peer_kernel, out_shape=(jax.ShapeDtypeStruct((4, r...  6.22 us
    pallas_call x1, Pallas kernels, project_own(): pl.pallas_call(project_own_kernel, out_shape=(part, part, part, part), gr...  5.99 us
    all_to_all x1, waiting for transfers between devices, shards(): lax.all_to_all(prompt, 'seq', 0, 0, tiled=True, axis_index_groups=[[i ^ K...  5.18 us
    ppermute x1, starting transfers between devices, shards(): last_a = lax.ppermute(next_a, 'mp', pair_b)  2.91 us
  transfers between devices with their start and end apart: 6, of which 4 were waited for; matrix products, arithmetic and copies ran while one was open for 5% of the time, Pallas kernels for 6%

profile of v5, /device:TPU:0, one launch (start us, length us, event | category | flops | bytes accessed | tf_op | source)
XLA Modules:
  0.0 94.1 jit_solution(10160442456396531192)
XLA Ops:
  0.6 6.2 %project_peer.1 = (bf16[4,512,512]{2,1,0:T(8,128)(2,1)}, s32[48]{0:T(128)}, bf16[16,2,128,256]{3,2,1,0:T(8,128)(2,1)}) custom-call(s32[1]{0:T(128)} %bitcast.z, s32[1]{0:T(128)} %bitcast.1.c, s32[1]{0:T(128)} %bitcast.2.here, bf16[576,512]{1,0:T(8,128)(2,1)} %bitcast.15, bf16[576,4096]{1,0:T(8,128)(2,1)} %bitcast.13, s32[128]{0:T(128)} %seq.1, s32[128]{0:T(128)} %pos.1, ...), custom_call_target="tpu_custom_call" | custom-call | flops 1207959552 | bytes 5242880 | tf_op jit(solution)/shard_map/project_peer/pallas_call | solution.py:125
  6.9 0.1 collective-permute-start
  7.0 7.1 %all-to-all-start = ((bf16[16,2,128,256]{3,2,1,0:T(8,128)(2,1)}), bf16[16,2,128,256]{3,2,1,0:T(8,128)(2,1)S(1)}, u32[]{:S(2)}, u32[]{:S(2)}) async-start(bf16[16,2,128,256]{3,2,1,0:T(8,128)(2,1)} %get-tuple-element.23), calls=%async_computation | async-start | bytes 4194304 | tf_op jit(solution)/shard_map/all_to_all | solution.py:423
  14.1 0.0 collective-permute-done.peer
  14.1 6.0 %project_own.1 = (bf16[2,512,256]{2,1,0:T(8,128)(2,1)}, bf16[2,512,256]{2,1,0:T(8,128)(2,1)}, bf16[2,512,256]{2,1,0:T(8,128)(2,1)}, bf16[2,512,256]{2,1,0:T(8,128)(2,1)}) custom-call(s32[1]{0:T(128)} %bitcast.z, s32[1]{0:T(128)} %bitcast.1.c, bf16[576,512]{1,0:T(8,128)(2,1)} %bitcast.16, bf16[576,4096]{1,0:T(8,128)(2,1)} %bitcast.14, ...), custom_call_target="tpu_custom_call" | custom-call | flops 1207959552 | bytes 7340032 | tf_op jit(solution)/shard_map/project_own/pallas_call | solution.py:187
  20.1 0.0 copy-start
  20.1 0.0 copy-start.1
  20.1 0.0 copy-start.2
  20.1 2.0 %collective-permute-start.1 = (bf16[2,512,256]{2,1,0:T(8,128)(2,1)}, bf16[2,512,256]{2,1,0:T(8,128)(2,1)S(1)}, u32[]{:S(2)}, u32[]{:S(2)}) collective-permute-start(bf16[2,512,256]{2,1,0:T(8,128)(2,1)} %get-tuple-element.26), channel_id=1, source_target_pairs={{0,2},{2,0},{4,6},{6,4},{1,3},{3,1},{5,7},{7,5},{8,10},{10,8},{12,... | collective-permute-start | bytes 1572872 | tf_op jit(solution)/shard_map/ppermute | solution.py:425
  22.1 2.5 %collective-permute-start.2 = (bf16[2,512,256]{2,1,0:T(8,128)(2,1)}, bf16[2,512,256]{2,1,0:T(8,128)(2,1)S(1)}, u32[]{:S(2)}, u32[]{:S(2)}) collective-permute-start(bf16[2,512,256]{2,1,0:T(8,128)(2,1)} %get-tuple-element.28), channel_id=1, source_target_pairs={{0,6},{2,4},{4,2},{6,0},{1,7},{3,5},{5,3},{7,1},{8,14},{10,12},{12... | collective-permute-start | bytes 1572872 | tf_op jit(solution)/shard_map/ppermute | solution.py:426
  24.6 10.0 %collective-permute-done.1 = bf16[2,512,256]{2,1,0:T(8,128)(2,1)S(1)} collective-permute-done((bf16[2,512,256]{2,1,0:T(8,128)(2,1)}, bf16[2,512,256]{2,1,0:T(8,128)(2,1)S(1)}, u32[]{:S(2)}, u32[]{:S(2)}) %collective-permute-start.1) | collective-permute-done | bytes 524320 | tf_op jit(solution)/shard_map/ppermute | solution.py:425
  34.6 1.7 %fusion = bf16[512,256]{1,0:T(8,128)(2,1)} fusion(bf16[2,512,256]{2,1,0:T(8,128)(2,1)S(1)} %collective-permute-done.1, bf16[2,512,256]{2,1,0:T(8,128)(2,1)} %get-tuple-element.29), kind=kLoop, calls=%fused_computation.4 | loop fusion | flops 524288 | bytes 786432 | tf_op jit(solution)/shard_map/convert_element_type | solution.py:427
  36.3 1.0 %collective-permute-done.2 = bf16[2,512,256]{2,1,0:T(8,128)(2,1)S(1)} collective-permute-done((bf16[2,512,256]{2,1,0:T(8,128)(2,1)}, bf16[2,512,256]{2,1,0:T(8,128)(2,1)S(1)}, u32[]{:S(2)}, u32[]{:S(2)}) %collective-permute-start.2) | collective-permute-done | bytes 524320 | tf_op jit(solution)/shard_map/ppermute | solution.py:426
  37.3 1.7 %fusion.1 = bf16[512,256]{1,0:T(8,128)(2,1)} fusion(bf16[2,512,256]{2,1,0:T(8,128)(2,1)S(1)} %collective-permute-done.2, bf16[2,512,256]{2,1,0:T(8,128)(2,1)} %get-tuple-element.32), kind=kLoop, calls=%fused_computation.5 | loop fusion | flops 524288 | bytes 786432 | tf_op jit(solution)/shard_map/convert_element_type | solution.py:428
  39.0 2.9 %collective-permute-start.3 = (bf16[512,256]{1,0:T(8,128)(2,1)}, bf16[512,256]{1,0:T(8,128)(2,1)S(1)}, u32[]{:S(2)}, u32[]{:S(2)}) collective-permute-start(bf16[512,256]{1,0:T(8,128)(2,1)} %fusion), channel_id=1, source_target_pairs={{0,6},{2,4},{4,2},{6,0},{1,7},{3,5},{5,3},{7,1},{8,14},{10,12},{12... | collective-permute-start | bytes 786440 | tf_op jit(solution)/shard_map/ppermute | solution.py:434
  41.9 0.0 collective-permute-start.4
  41.9 1.2 %fusion.2 = (bf16[512,256]{1,0:T(8,128)(2,1)S(1)}, bf16[512,256]{1,0:T(8,128)(2,1)S(1)}) fusion(bf16[2,512,256]{2,1,0:T(8,128)(2,1)S(1)} %collective-permute-done.1, bf16[2,512,256]{2,1,0:T(8,128)(2,1)} %get-tuple-element.29, bf16[2,512,256]{2,1,0:T(8,128)(2,1)S(1)} %collective-permute-done.2, bf16[2,512,256]{2,1,0:T(8,128)(2,1)} %get-tuple-element.32), kind=kLoop, calls=%fused_computation.6 | loop fusion | flops 1048576 | bytes 1572864 | tf_op jit(solution)/shard_map/convert_element_type | solution.py:432
  43.1 5.2 %all-to-all-done.gathered = bf16[16,2,128,256]{3,2,1,0:T(8,128)(2,1)S(1)} async-done(((bf16[16,2,128,256]{3,2,1,0:T(8,128)(2,1)}), bf16[16,2,128,256]{3,2,1,0:T(8,128)(2,1)S(1)}, u32[]{:S(2)}, u32[]{:S(2)}) %all-to-all-start) | async-done | bytes 2097184 | tf_op jit(solution)/shard_map/all_to_all | solution.py:423
  48.3 0.0 collective-permute-done.3.last_a
  48.3 1.3 %collective-permute-done.4.last_b = bf16[512,256]{1,0:T(8,128)(2,1)} collective-permute-done((bf16[512,256]{1,0:T(8,128)(2,1)}, bf16[512,256]{1,0:T(8,128)(2,1)}, u32[]{:S(2)}, u32[]{:S(2)}) %collective-permute-start.4) | collective-permute-done | bytes 262176 | tf_op jit(solution)/shard_map/ppermute | solution.py:435
  49.5 0.0 copy-done
  49.5 0.0 copy-done.1
  49.5 0.0 copy-done.2
  49.6 0.0 copy-start.3
  49.6 1.0 %copy-done.3 = bf16[512,512]{1,0:T(8,128)(2,1)S(1)} copy-done((bf16[512,512]{1,0:T(8,128)(2,1)S(1)}, bf16[512,512]{1,0:T(8,128)(2,1)}, u32[]{:S(2)}) %copy-start.3) | copy-done | bytes 524312
  50.6 12.2 %attend.1 = (bf16[512,512]{1,0:T(8,128)(2,1)}, bf16[512,256]{1,0:T(8,128)(2,1)S(1)}, bf16[512,256]{1,0:T(8,128)(2,1)S(1)}, bf16[16,2,128,256]{3,2,1,0:T(8,128)(2,1)S(1)}) custom-call(s32[48]{0:T(128)S(1)} %copy-done.2, bf16[512,512]{1,0:T(8,128)(2,1)S(1)} %copy-done.3, bf16[512,256]{1,0:T(8,128)(2,1)S(1)} %copy-done, bf16[512,256]{1,0:T(8,128)(2,1)S(1)} %copy-done.1, ...), custom_call_target="tpu_custom_call" | custom-call | flops 4000000000 | bytes 8388608 | tf_op jit(solution)/shard_map/attend/pallas_call | solution.py:343
  62.8 29.7 %all_to_all.10.ret = bf16[16,2,128,256]{3,2,1,0:T(8,128)(2,1)S(1)} all-to-all(bf16[16,2,128,256]{3,2,1,0:T(8,128)(2,1)S(1)} %get-tuple-element.38), channel_id=1, replica_groups={{80,88,64,72,112,120,96,104,16,24,0,8,48,56,32,40},{81,89,65,73,113,121..., dimensions={0} | all-to-all | bytes 4194304 | tf_op jit(solution)/shard_map/all_to_all | solution.py:438
  92.5 1.7 %finish.1 = (bf16[512,256]{1,0:T(8,128)(2,1)}, bf16[512,256]{1,0:T(8,128)(2,1)}) custom-call(s32[48]{0:T(128)S(1)} %copy-done.2, bf16[512,256]{1,0:T(8,128)(2,1)S(1)} %get-tuple-element.36.own_k, bf16[512,256]{1,0:T(8,128)(2,1)S(1)} %get-tuple-element.37.own_v, bf16[16,2,128,256]{3,2,1,0:T(8,128)(2,1)S(1)} %all_to_all.10.ret), custom_call_target="tpu_custom_call" | custom-call | tf_op jit(solution)/shard_map/finish/pallas_call | solution.py:400
Async XLA Ops:
  6.9 7.2 %collective-permute-start = (bf16[4,512,512]{2,1,0:T(8,128)(2,1)}, bf16[4,512,512]{2,1,0:T(8,128)(2,1)}, u32[]{:S(2)}, u32[]{:S(2)}) collective-permute-start(bf16[4,512,512]{2,1,0:T(8,128)(2,1)} %get-tuple-element.24), channel_id=1, source_target_pairs={{0,1},{1,0},{2,3},{3,2},{4,5},{5,4},{6,7},{7,6},{8,9},{9,8},{10,11... | collective-permute-start | bytes 6291464 | tf_op jit(solution)/shard_map/ppermute | solution.py:422
  7.0 41.3 %all-to-all-start = ((bf16[16,2,128,256]{3,2,1,0:T(8,128)(2,1)}), bf16[16,2,128,256]{3,2,1,0:T(8,128)(2,1)S(1)}, u32[]{:S(2)}, u32[]{:S(2)}) async-start(bf16[16,2,128,256]{3,2,1,0:T(8,128)(2,1)} %get-tuple-element.23), calls=%async_computation | async-start | bytes 4194304 | tf_op jit(solution)/shard_map/all_to_all | solution.py:423
  20.1 29.4 %copy-start = (bf16[512,256]{1,0:T(8,128)(2,1)S(1)}, bf16[512,256]{1,0:T(8,128)(2,1)}, u32[]{:S(2)}) copy-start(bf16[512,256]{1,0:T(8,128)(2,1)} %k.1) | copy-start | bytes 786436
  20.1 29.4 %copy-start.1 = (bf16[512,256]{1,0:T(8,128)(2,1)S(1)}, bf16[512,256]{1,0:T(8,128)(2,1)}, u32[]{:S(2)}) copy-start(bf16[512,256]{1,0:T(8,128)(2,1)} %v.1) | copy-start | bytes 786436
  20.1 29.4 %copy-start.2 = (s32[48]{0:T(128)S(1)}, s32[48]{0:T(128)}, u32[]{:S(2)}) copy-start(s32[48]{0:T(128)} %get-tuple-element.22.meta) | copy-start | bytes 580
  20.1 14.5 %collective-permute-start.1 = (bf16[2,512,256]{2,1,0:T(8,128)(2,1)}, bf16[2,512,256]{2,1,0:T(8,128)(2,1)S(1)}, u32[]{:S(2)}, u32[]{:S(2)}) collective-permute-start(bf16[2,512,256]{2,1,0:T(8,128)(2,1)} %get-tuple-element.26), channel_id=1, source_target_pairs={{0,2},{2,0},{4,6},{6,4},{1,3},{3,1},{5,7},{7,5},{8,10},{10,8},{12,... | collective-permute-start | bytes 1572872 | tf_op jit(solution)/shard_map/ppermute | solution.py:425
  22.1 15.2 %collective-permute-start.2 = (bf16[2,512,256]{2,1,0:T(8,128)(2,1)}, bf16[2,512,256]{2,1,0:T(8,128)(2,1)S(1)}, u32[]{:S(2)}, u32[]{:S(2)}) collective-permute-start(bf16[2,512,256]{2,1,0:T(8,128)(2,1)} %get-tuple-element.28), channel_id=1, source_target_pairs={{0,6},{2,4},{4,2},{6,0},{1,7},{3,5},{5,3},{7,1},{8,14},{10,12},{12... | collective-permute-start | bytes 1572872 | tf_op jit(solution)/shard_map/ppermute | solution.py:426
  39.0 9.3 %collective-permute-start.3 = (bf16[512,256]{1,0:T(8,128)(2,1)}, bf16[512,256]{1,0:T(8,128)(2,1)S(1)}, u32[]{:S(2)}, u32[]{:S(2)}) collective-permute-start(bf16[512,256]{1,0:T(8,128)(2,1)} %fusion), channel_id=1, source_target_pairs={{0,6},{2,4},{4,2},{6,0},{1,7},{3,5},{5,3},{7,1},{8,14},{10,12},{12... | collective-permute-start | bytes 786440 | tf_op jit(solution)/shard_map/ppermute | solution.py:434
  41.9 7.6 %collective-permute-start.4 = (bf16[512,256]{1,0:T(8,128)(2,1)}, bf16[512,256]{1,0:T(8,128)(2,1)}, u32[]{:S(2)}, u32[]{:S(2)}) collective-permute-start(bf16[512,256]{1,0:T(8,128)(2,1)} %fusion.1), channel_id=1, source_target_pairs={{0,2},{2,0},{4,6},{6,4},{1,3},{3,1},{5,7},{7,5},{8,10},{10,8},{12,... | collective-permute-start | bytes 786440 | tf_op jit(solution)/shard_map/ppermute | solution.py:435
  49.6 1.0 %copy-start.3 = (bf16[512,512]{1,0:T(8,128)(2,1)S(1)}, bf16[512,512]{1,0:T(8,128)(2,1)}, u32[]{:S(2)}) copy-start(bf16[512,512]{1,0:T(8,128)(2,1)} %q.1) | copy-start | bytes 1572868
